TPU v7x, 256 devices: a whole 4x4x8 slice. The times are simulated.
256 devices in a mesh: gx: 128 (over z, x, y), gy: 2 (over core).
Axes of the slice: x: 4, y: 4, z: 8, core: 2. Of those that a mesh axis runs over, the one named last changes fastest.
Arguments:
- log_perm: float32 [4, 128, 256, 256], P(None, 'gx', None, 'gy'), may hold values from -4 to 4
- recharge: float32 [4, 256, 256], P(None, None, 'gy'), may hold values from -24 to 24
- well_cells: int32 [32], replicated, may hold values from 0 to 262143
- observed: float32 [32], replicated, may hold values from -5 to 5
- variances: float32 [32], replicated, may hold values from 0.02 to 0.2
- well_order: int32 [8], replicated, may hold values from 0 to 31
Outputs:
- post_perm: float32 [4, 128, 256, 256], P(None, None, 'gx', 'gy')
- post_head: float32 [4, 128, 256, 256], P(None, None, 'gx', 'gy')
Inputs may be any that keep to these rules, and one draw needn't show every extreme that they name: `well_cells`: each entry is a flat cell index layer * 256 * 256 + row * 256 + column; wells may share a cell. `well_order`: wells may repeat or be absent.
All inputs are finite; a program needn't handle non-finite values.
Results may differ from a plain program's by a relative error of at most 0.0003.
Values sent between devices are 32-bit elements; how exact they have to be, the bound alone decides.
No kernel may reach another device: no remote copies, remote signals or barrier semaphores. Data moves between devices by JAX's collectives and lax.ppermute only.
A program may use at most 64 MiB of HBM per device.

v0:
```python
import jax
import jax.numpy as jnp
from jax import lax
from jax.sharding import PartitionSpec as P

PASSES = 8
STEPS = 8


VERT = 0.1
LEAK = 0.1


def extended(cells, sides, width):
    for axis, dim in sides:
        count = lax.axis_size(axis)
        ends = count - 1
        head = lax.slice_in_dim(cells, 0, width, axis=dim)
        tail = lax.slice_in_dim(cells, cells.shape[dim] - width, cells.shape[dim], axis=dim)
        cells = jnp.concatenate(
            [
                lax.ppermute(tail, axis, [(i, (i + 1) % count) for i in range(ends)]),
                cells,
                lax.ppermute(head, axis, [((i + 1) % count, i) for i in range(ends)]),
            ],
            axis=dim,
        )
    return cells


def spread_2(x, axis, root):
    mine = lax.axis_index(axis) == root
    return lax.psum(jnp.where(mine, x, jnp.zeros_like(x)), axis)


def harmonic(first, second):
    return 2.0 * first * second / (first + second)


def coefficients(centre, padded):
    north = harmonic(centre, padded[:, :, :-2, 1:-1])
    south = harmonic(centre, padded[:, :, 2:, 1:-1])
    west = harmonic(centre, padded[:, :, 1:-1, :-2])
    east = harmonic(centre, padded[:, :, 1:-1, 2:])
    vertical = VERT * harmonic(centre[1:], centre[:-1])
    zero_layer = jnp.zeros_like(centre[:1])
    upper = jnp.concatenate([zero_layer, vertical], 0)
    lower = jnp.concatenate([vertical, zero_layer], 0)
    diagonal = LEAK + north + south + west + east + upper + lower
    return (north, south, west, east, upper, lower, diagonal)


def relax(head_pad, head, coef, source):
    north, south, west, east, upper, lower, diagonal = coef
    zero_layer = jnp.zeros_like(head[:1])
    total = north * head_pad[:, :, :-2, 1:-1] + south * head_pad[:, :, 2:, 1:-1]
    total = total + west * head_pad[:, :, 1:-1, :-2] + east * head_pad[:, :, 1:-1, 2:]
    total = total + upper * jnp.concatenate([zero_layer, head[:-1]], 0)
    total = total + lower * jnp.concatenate([head[1:], zero_layer], 0)
    return (source + total) / diagonal


def well_terms(row, obs_value, variance):
    members = row.shape[0]
    mean_value = jnp.mean(row)
    spread = row - mean_value
    denom = jnp.sum(spread * spread) / (members - 1) + variance
    alpha = 1.0 / (1.0 + jnp.sqrt(variance / denom))
    weights = obs_value - mean_value - alpha * spread
    factor = 1.0 / ((members - 1) * denom)
    return (spread, factor, weights)


def assimilate_field(field, spread, factor, weights):
    covar = jnp.einsum("lmrc,m->lrc", field, spread, precision=lax.Precision.HIGHEST)
    return field + (covar * factor)[:, None] * weights[None, :, None, None]


def body(log_perm, recharge, well_cells, observed, variances, well_order):
    columns = log_perm.shape[3]
    perm_edge = extended(log_perm, (("gy", 3),), 1)
    padded = jnp.exp(jnp.pad(perm_edge, ((0, 0), (0, 0), (1, 1), (0, 0))))
    coef = coefficients(jnp.exp(log_perm), padded)
    source = recharge[:, None]
    head = jnp.zeros_like(log_perm)
    for sweep in range(PASSES):
        edged = extended(head, (("gy", 3),), 1)
        head = relax(jnp.pad(edged, ((0, 0), (0, 0), (1, 1), (0, 0))), head, coef, source)
    perm_rows, head_rows = (
        lax.all_to_all(log_perm, "gx", split_axis=2, concat_axis=1, tiled=True),
        lax.all_to_all(head, "gx", split_axis=2, concat_axis=1, tiled=True),
    )
    members = head_rows.shape[1]
    rows_local = head_rows.shape[2]
    row_place = lax.axis_index("gx")
    col_place = lax.axis_index("gy")
    total_rows = rows_local * lax.axis_size("gx")
    total_cols = columns * lax.axis_size("gy")

    def locate(index):
        layer = index // (total_rows * total_cols)
        row = index // total_cols % total_rows
        column = index % total_cols
        local_row = jnp.clip(row - row_place * rows_local, 0, rows_local - 1)
        local_col = jnp.clip(column - col_place * columns, 0, columns - 1)
        return (layer, row, column, local_row, local_col)

    def step_single(k, carry):
        perm_state, head_state = carry
        well = well_order[k]
        layer, row, column, local_row, local_col = locate(well_cells[well])
        zero_index = jnp.int32(0)
        candidate = lax.dynamic_slice(
            head_state, (layer, zero_index, local_row, local_col), (1, members, 1, 1)
        ).reshape(members)
        owner = row // rows_local * lax.axis_size("gy") + column // columns
        values = spread_2(candidate, ("gx", "gy"), owner)
        spread, factor, weights = well_terms(values, observed[well], variances[well])
        perm_state = assimilate_field(perm_state, spread, factor, weights)
        head_state = assimilate_field(head_state, spread, factor, weights)
        return (perm_state, head_state)

    post_perm, post_head = lax.fori_loop(0, STEPS, step_single, (perm_rows, head_rows))
    return (post_perm, post_head)


def solution(mesh):
    placed = (P(None, "gx", None, "gy"), P(None, None, "gy"), P(), P(), P(), P())
    return jax.shard_map(
        body,
        mesh=mesh,
        in_specs=placed,
        out_specs=(P(None, None, "gx", "gy"), P(None, None, "gx", "gy")),
        check_vma=False,
    )
```

profile of v0, /device:TPU:1, one launch (start us, length us, event | category | flops | bytes accessed | tf_op | source)
XLA Modules:
  0.0 829.1 jit_solution(13846620547306406823)
XLA Ops:
  0.7 1.3 collective-permute-start.2
  2.0 5.2 collective-permute-start.3
  7.2 2.3 copy_exponential_fusion
  9.5 14.2 %all-to-all-start = ((f32[4,1,256,128]{3,0,1,2:T(4,128)}), f32[4,1,256,128]{3,0,1,2:T(4,128)S(1)}, u32[]{:S(2)}, u32[]{:S(2)}) async-start(f32[4,1,256,128]{3,0,1,2:T(4,128)} %get-tuple-element.357), calls=%async_computation | async-start | bytes 1048576 | tf_op jit(solution)/shard_map/all_to_all | solution.py:90
  23.8 1.6 fusion.94
  25.3 1.3 collective-permute-start
  26.6 3.1 collective-permute-start.1
  30.0 1.2 collective-permute-done.1
  31.2 1.9 fusion.5
  33.3 0.9 select_maximum_fusion.14
  34.5 2.4 fusion.13
  37.2 1.3 collective-permute-start.4
  38.5 3.1 collective-permute-start.5
  41.8 1.3 collective-permute-done.5
  43.1 0.9 select_maximum_fusion.12
  43.9 1.6 fusion.74
  45.9 1.3 collective-permute-start.6
  47.2 3.3 collective-permute-start.7
  50.7 1.1 collective-permute-done.7
  51.8 0.9 select_maximum_fusion.10
  52.6 1.6 fusion.65
  54.6 1.3 collective-permute-start.8
  55.9 3.1 collective-permute-start.9
  59.2 1.3 collective-permute-done.9
  60.4 0.9 select_maximum_fusion.8
  61.3 1.6 fusion.56
  63.3 1.3 collective-permute-start.10
  64.5 3.1 collective-permute-start.11
  67.9 1.3 collective-permute-done.11
  69.1 0.9 select_maximum_fusion.6
  70.0 1.6 fusion.47
  71.9 1.3 collective-permute-start.12
  73.2 3.3 collective-permute-start.13
  76.8 1.0 collective-permute-done.13
  77.8 0.9 select_maximum_fusion.4
  78.7 1.6 fusion.38
  80.6 1.3 collective-permute-start.14
  81.9 3.1 collective-permute-start.15
  85.2 1.3 collective-permute-done.15
  86.5 0.9 select_maximum_fusion.2
  87.4 1.6 fusion.29
  89.3 1.3 collective-permute-start.16
  90.6 3.1 collective-permute-start.17
  93.9 1.3 collective-permute-done.17
  95.2 0.9 select_maximum_fusion
  96.1 2.3 fusion.20
  98.4 13.4 %all-to-all-start.1 = ((f32[4,1,256,128]{3,0,1,2:T(4,128)}), f32[4,1,256,128]{3,0,1,2:T(4,128)S(1)}, u32[]{:S(2)}, u32[]{:S(2)}) async-start(f32[4,1,256,128]{3,0,1,2:T(4,128)} %fusion.20), calls=%async_computation.1 | async-start | bytes 1048576 | tf_op jit(solution)/shard_map/all_to_all | solution.py:91
  112.1 18.3 %all-to-all-done.1 = f32[4,1,256,128]{3,0,1,2:T(4,128)S(1)} async-done(((f32[4,1,256,128]{3,0,1,2:T(4,128)}), f32[4,1,256,128]{3,0,1,2:T(4,128)S(1)}, u32[]{:S(2)}, u32[]{:S(2)}) %all-to-all-start.1) | async-done | bytes 524320 | tf_op jit(solution)/shard_map/all_to_all | solution.py:91
  130.7 696.4 %while.18 = (s32[]{:T(128)}, f32[4,128,2,128]{1,3,2,0:T(8,128)S(1)}, f32[4,128,2,128]{1,3,2,0:T(8,128)S(1)}, s32[8]{0:T(128)S(1)}, s32[32]{0:T(128)S(1)}, /*inde...) while((s32[]{:T(128)}, ...), condition=%wide.region_4.5_spmd, body=%wide.region_0.4_spmd.sunk | while | flops 3673189 | bytes 3186046 | solution.py:123
  136.5 73.7 %psum.16 = f32[128]{0:T(128)S(1)} all-reduce(f32[128]{0:T(128)S(1)} %fusion.108), channel_id=1, replica_groups=mesh['gx'=128,'gy'=2] {'gx','gy'}, use_global_device_ids=true, to_apply=%region_1.1 | all-reduce | flops 128 | bytes 1024 | tf_op jit(solution)/shard_map/while/body/eval_jaxpr/psum | solution.py:33
  211.5 0.6 multiply_reduce_fusion.2
  223.4 74.3 %psum.16 = f32[128]{0:T(128)S(1)} all-reduce(f32[128]{0:T(128)S(1)} %fusion.108), channel_id=1, replica_groups=mesh['gx'=128,'gy'=2] {'gx','gy'}, use_global_device_ids=true, to_apply=%region_1.1 | all-reduce | flops 128 | bytes 1024 | tf_op jit(solution)/shard_map/while/body/eval_jaxpr/psum | solution.py:33
  299.0 0.6 multiply_reduce_fusion.2
  310.9 73.4 %psum.16 = f32[128]{0:T(128)S(1)} all-reduce(f32[128]{0:T(128)S(1)} %fusion.108), channel_id=1, replica_groups=mesh['gx'=128,'gy'=2] {'gx','gy'}, use_global_device_ids=true, to_apply=%region_1.1 | all-reduce | flops 128 | bytes 1024 | tf_op jit(solution)/shard_map/while/body/eval_jaxpr/psum | solution.py:33
  385.6 0.6 multiply_reduce_fusion.2
  397.5 74.2 %psum.16 = f32[128]{0:T(128)S(1)} all-reduce(f32[128]{0:T(128)S(1)} %fusion.108), channel_id=1, replica_groups=mesh['gx'=128,'gy'=2] {'gx','gy'}, use_global_device_ids=true, to_apply=%region_1.1 | all-reduce | flops 128 | bytes 1024 | tf_op jit(solution)/shard_map/while/body/eval_jaxpr/psum | solution.py:33
  473.0 0.6 multiply_reduce_fusion.2
  484.9 73.5 %psum.16 = f32[128]{0:T(128)S(1)} all-reduce(f32[128]{0:T(128)S(1)} %fusion.108), channel_id=1, replica_groups=mesh['gx'=128,'gy'=2] {'gx','gy'}, use_global_device_ids=true, to_apply=%region_1.1 | all-reduce | flops 128 | bytes 1024 | tf_op jit(solution)/shard_map/while/body/eval_jaxpr/psum | solution.py:33
  559.6 0.6 multiply_reduce_fusion.2
  571.6 74.2 %psum.16 = f32[128]{0:T(128)S(1)} all-reduce(f32[128]{0:T(128)S(1)} %fusion.108), channel_id=1, replica_groups=mesh['gx'=128,'gy'=2] {'gx','gy'}, use_global_device_ids=true, to_apply=%region_1.1 | all-reduce | flops 128 | bytes 1024 | tf_op jit(solution)/shard_map/while/body/eval_jaxpr/psum | solution.py:33
  659.0 73.4 %psum.16 = f32[128]{0:T(128)S(1)} all-reduce(f32[128]{0:T(128)S(1)} %fusion.108), channel_id=1, replica_groups=mesh['gx'=128,'gy'=2] {'gx','gy'}, use_global_device_ids=true, to_apply=%region_1.1 | all-reduce | flops 128 | bytes 1024 | tf_op jit(solution)/shard_map/while/body/eval_jaxpr/psum | solution.py:33
  745.5 74.3 %psum.16 = f32[128]{0:T(128)S(1)} all-reduce(f32[128]{0:T(128)S(1)} %fusion.108), channel_id=1, replica_groups=mesh['gx'=128,'gy'=2] {'gx','gy'}, use_global_device_ids=true, to_apply=%region_1.1 | all-reduce | flops 128 | bytes 1024 | tf_op jit(solution)/shard_map/while/body/eval_jaxpr/psum | solution.py:33
  827.1 1.0 copy.33
  828.1 1.0 copy.34
  (135 shorter events, 42.9 us)
Async XLA Ops:
  0.7 32.5 %collective-permute-start.2 = (f32[4,1,256,1]{3,0,1,2:T(4,128)S(1)}, f32[4,1,256,1]{3,0,1,2:T(4,128)S(1)}, u32[]{:S(2)}, u32[]{:S(2)}) collective-permute-start(f32[4,1,256,1]{3,0,1,2:T(4,128)S(1)} %broadcast.95), channel_id=1, source_target_pairs={{0,1},{2,3},{4,5},{6,7},{8,9},{10,11},{12,13},{14,15},{16,17},{18,... | collective-permute-start | bytes 12296 | tf_op jit(solution)/shard_map/ppermute | solution.py:22
  2.0 31.2 %collective-permute-start.3 = (f32[4,1,256,1]{3,0,1,2:T(4,128)S(1)}, f32[4,1,256,1]{3,0,1,2:T(4,128)S(1)}, u32[]{:S(2)}, u32[]{:S(2)}) collective-permute-start(f32[4,1,256,1]{3,0,1,2:T(4,128)S(1)} %broadcast.95), channel_id=1, source_target_pairs={{1,0},{3,2},{5,4},{7,6},{9,8},{11,10},{13,12},{15,14},{17,16},{19,... | collective-permute-start | bytes 12296 | tf_op jit(solution)/shard_map/ppermute | solution.py:24
  9.5 88.9 %all-to-all-start = ((f32[4,1,256,128]{3,0,1,2:T(4,128)}), f32[4,1,256,128]{3,0,1,2:T(4,128)S(1)}, u32[]{:S(2)}, u32[]{:S(2)}) async-start(f32[4,1,256,128]{3,0,1,2:T(4,128)} %get-tuple-element.357), calls=%async_computation | async-start | bytes 1048576 | tf_op jit(solution)/shard_map/all_to_all | solution.py:90
  25.3 4.7 collective-permute-start
  26.6 4.6 collective-permute-start.1
  33.3 1.0 copy-start
  33.3 1.2 copy-start.1
  37.2 4.6 collective-permute-start.4
  38.5 4.6 collective-permute-start.5
  45.9 4.8 collective-permute-start.6
  47.2 4.6 collective-permute-start.7
  54.6 4.6 collective-permute-start.8
  55.9 4.6 collective-permute-start.9
  63.3 4.6 collective-permute-start.10
  64.5 4.6 collective-permute-start.11
  71.9 4.8 collective-permute-start.12
  73.2 4.6 collective-permute-start.13
  80.6 4.6 collective-permute-start.14
  81.9 4.6 collective-permute-start.15
  89.3 4.6 collective-permute-start.16
  90.6 4.6 collective-permute-start.17
  98.4 32.0 %all-to-all-start.1 = ((f32[4,1,256,128]{3,0,1,2:T(4,128)}), f32[4,1,256,128]{3,0,1,2:T(4,128)S(1)}, u32[]{:S(2)}, u32[]{:S(2)}) async-start(f32[4,1,256,128]{3,0,1,2:T(4,128)} %fusion.20), calls=%async_computation.1 | async-start | bytes 1048576 | tf_op jit(solution)/shard_map/all_to_all | solution.py:91
  111.8 18.8 %copy-start.2 = (s32[8]{0:T(128)S(1)}, s32[8]{0:T(128)}, u32[]{:S(2)}) copy-start(s32[8]{0:T(128)} %param.13) | copy-start | bytes 100
  111.9 18.8 %copy-start.3 = (s32[32]{0:T(128)S(1)}, s32[32]{0:T(128)}, u32[]{:S(2)}) copy-start(s32[32]{0:T(128)} %param.10) | copy-start | bytes 388
  111.9 18.8 %copy-start.4 = (f32[32]{0:T(128)S(1)}, f32[32]{0:T(128)}, u32[]{:S(2)}) copy-start(f32[32]{0:T(128)} %param.12) | copy-start | bytes 388
  111.9 18.8 %copy-start.5 = (f32[32]{0:T(128)S(1)}, f32[32]{0:T(128)}, u32[]{:S(2)}) copy-start(f32[32]{0:T(128)} %param.11) | copy-start | bytes 388
where the time goes:
time: 832 us; the launch traced here: 829 us
  blocking collectives  591 us (71%)
  starting transfers between devices  69.6 us (8%)
  loops' own time  64.6 us (8%)
  other arithmetic  37.1 us (4%)
  local copies, waits for them, and re-layouts  29.4 us (4%)
  waiting for transfers between devices  27.9 us (3%)
  matrix products  8.36 us (1%)
    psum x8, blocking collectives, spread_2(): return lax.psum(jnp.where(mine, x, jnp.zeros_like(x)), axis)  591 us
    another operation x1, loops' own time, body(): lax.fori_loop(0, STEPS, step_single, (perm_rows, head_rows))  64.6 us
    ppermute x9, starting transfers between devices, extended(): lax.ppermute(head, axis, [((i + 1) % count, i) for i in range(ends)])  30.3 us
    all_to_all x1, waiting for transfers between devices, body(): lax.all_to_all(head, 'gx', split_axis=2, concat_axis=1, tiled=True)  18.3 us
  transfers between devices with their start and end apart: 20, of which 9 were waited for; matrix products, arithmetic and copies ran while one was open for 4% of the time, Pallas kernels for 0%

commit v1 on v0

v1 whole, which is shorter than its diff:
```python
import functools

import jax
import jax.numpy as jnp
from jax import lax
from jax.experimental import pallas as pl
from jax.experimental.pallas import tpu as pltpu
from jax.sharding import PartitionSpec as P

PASSES = 8
STEPS = 8
VERT = 0.1
LEAK = 0.1
HALO = 8
PAD = 8
CHUNK = 32
HIGHEST = lax.Precision.HIGHEST

VMEM = pl.BlockSpec(memory_space=pltpu.VMEM)
SMEM = pl.BlockSpec(memory_space=pltpu.SMEM)
PARAMS = pltpu.CompilerParams(vmem_limit_bytes=48 * 1024 * 1024)


def edges_kernel(core_ref, perm_ref, rech_ref, near_ref, away_ref):
    layers, rows, columns = perm_ref.shape
    core = core_ref[0]
    lane = lax.broadcasted_iota(jnp.int32, (2 * HALO, columns), 1)
    slot = lax.broadcasted_iota(jnp.int32, (2 * HALO, columns), 0)
    depth = jnp.where(slot < HALO, slot, 2 * HALO - 1 - slot)
    wanted = jnp.where(core == 0, columns - 1 - depth, depth)
    pick = (lane == wanted).astype(jnp.float32)
    for which, ref in enumerate((perm_ref, rech_ref)):
        for layer in range(layers):
            both = lax.dot_general(
                pick, ref[layer], (((1,), (1,)), ((), ())), precision=HIGHEST,
                preferred_element_type=jnp.float32,
            )
            near_ref[which, layer] = both[:HALO]
            away_ref[which, layer] = both[HALO:]


def pack_rows(load, send_ref, layers, rows, stride):
    for layer in range(layers):
        for r in range(2):
            for g in range(0, rows // 2, 8):
                send_ref[pl.ds(stride * g + 2 * layer + r, 8, stride=stride), :] = load(layer, 2 * g + r)


def pack_kernel(perm_ref, send_ref):
    layers, rows, _ = perm_ref.shape
    pack_rows(
        lambda layer, start: perm_ref[layer, pl.ds(start, 8, stride=2), :],
        send_ref, layers, rows, 2 * layers,
    )


def harmonic_inv(a, b):
    return 2.0 / (a + b)


def strip_heads(near_ref, far_ref):
    layers = near_ref.shape[1]
    rows = near_ref.shape[3]
    lane = lax.broadcasted_iota(jnp.int32, (2 * HALO, rows), 1)
    first, last = lane == 0, lane == rows - 1
    inv, source = [], []
    for layer in range(layers):
        inv.append(jnp.exp(-jnp.concatenate([far_ref[0, layer], near_ref[0, layer]], 0)))
        source.append(jnp.concatenate([far_ref[1, layer], near_ref[1, layer]], 0))
    vertical = [VERT * harmonic_inv(inv[i], inv[i + 1]) for i in range(layers - 1)]
    coef = []
    for layer in range(layers):
        a = inv[layer]
        north = harmonic_inv(a, jnp.where(first, 1.0, pltpu.roll(a, 1, 1)))
        south = harmonic_inv(a, jnp.where(last, 1.0, pltpu.roll(a, rows - 1, 1)))
        west = harmonic_inv(a, pltpu.roll(a, 1, 0))
        east = harmonic_inv(a, pltpu.roll(a, 2 * HALO - 1, 0))
        diag = LEAK + north + south + west + east
        if layer > 0:
            diag = diag + vertical[layer - 1]
        if layer < layers - 1:
            diag = diag + vertical[layer]
        scale = 1.0 / diag
        terms = [
            jnp.where(first, 0.0, north * scale), jnp.where(last, 0.0, south * scale),
            west * scale, east * scale,
            vertical[layer - 1] * scale if layer > 0 else None,
            vertical[layer] * scale if layer < layers - 1 else None,
            source[layer] * scale,
        ]
        coef.append(terms)
    head = [coef[layer][6] for layer in range(layers)]
    kept = [head[layer][HALO - 1:HALO] for layer in range(layers)]
    for _ in range(PASSES - 2):
        fresh = []
        for layer in range(layers):
            north, south, west, east, upper, lower, base = coef[layer]
            h = head[layer]
            total = base + north * pltpu.roll(h, 1, 1) + south * pltpu.roll(h, rows - 1, 1)
            total = total + west * pltpu.roll(h, 1, 0) + east * pltpu.roll(h, 2 * HALO - 1, 0)
            if upper is not None:
                total = total + upper * head[layer - 1]
            if lower is not None:
                total = total + lower * head[layer + 1]
            fresh.append(total)
        head = fresh
        kept += [head[layer][HALO - 1:HALO] for layer in range(layers)]
    kept += [inv[layer][HALO - 1:HALO] for layer in range(layers)]
    return jnp.concatenate(kept, 0)


def jacobi_kernel(
    core_ref, cells_ref, order_ref, perm_ref, rech_ref, near_ref, far_ref,
    send_ref,
    inv, rowt, vert, cn, cs, cw, ce, cu, cd, base, head_a, head_b, halo,
):
    layers, rows, columns = perm_ref.shape
    core = core_ref[0]
    stripe = lax.broadcasted_iota(jnp.int32, (CHUNK, columns), 1)
    west_cut = jnp.logical_and(stripe == 0, core == 1)
    east_cut = jnp.logical_and(stripe == columns - 1, core == 0)
    west_end = jnp.logical_and(stripe == 0, core == 0)
    east_end = jnp.logical_and(stripe == columns - 1, core == 1)
    edge_lane = jnp.where(core == 0, columns - 1, 0)

    kept = strip_heads(near_ref, far_ref)
    count = kept.shape[0]
    halo[...] = jnp.concatenate([kept, jnp.zeros((columns - count, rows), jnp.float32)], 0).T

    def shift_of(index):
        return lax.rem(edge_lane - index + columns, columns)

    ones = jnp.ones((PAD, columns), jnp.float32)
    zeros = jnp.zeros((PAD, columns), jnp.float32)
    for layer in range(layers):
        inv[layer, 0:PAD, :] = ones
        inv[layer, PAD + rows:2 * PAD + rows, :] = ones
        for ref in (head_a, head_b):
            ref[layer, 0:PAD, :] = zeros
            ref[layer, PAD + rows:2 * PAD + rows, :] = zeros
        for r in range(0, rows, CHUNK):
            inv[layer, PAD + r:PAD + r + CHUNK, :] = jnp.exp(-perm_ref[layer, r:r + CHUNK, :])
    for layer in range(layers):
        rowt[layer, 0:PAD, :] = harmonic_inv(inv[layer, 0:PAD, :], inv[layer, 1:PAD + 1, :])
        for r in range(0, rows, CHUNK):
            here = inv[layer, PAD + r:PAD + r + CHUNK, :]
            rowt[layer, PAD + r:PAD + r + CHUNK, :] = harmonic_inv(
                here, inv[layer, PAD + r + 1:PAD + r + CHUNK + 1, :]
            )
            if layer < layers - 1:
                vert[layer, r:r + CHUNK, :] = VERT * harmonic_inv(
                    here, inv[layer + 1, PAD + r:PAD + r + CHUNK, :]
                )
    for layer in range(layers):
        shift = shift_of(count - layers + layer)
        for r in range(0, rows, CHUNK):
            part = pl.ds(r, CHUNK)
            here = inv[layer, PAD + r:PAD + r + CHUNK, :]
            beyond = pltpu.roll(halo[part, :], shift, 1)
            inv_w = jnp.where(west_cut, beyond, jnp.where(west_end, 1.0, pltpu.roll(here, 1, 1)))
            inv_e = jnp.where(east_cut, beyond, jnp.where(east_end, 1.0, pltpu.roll(here, columns - 1, 1)))
            west = harmonic_inv(here, inv_w)
            east = harmonic_inv(here, inv_e)
            north = rowt[layer, PAD + r - 1:PAD + r + CHUNK - 1, :]
            south = rowt[layer, PAD + r:PAD + r + CHUNK, :]
            diag = LEAK + north + south + west + east
            if layer > 0:
                diag = diag + vert[layer - 1, part, :]
            if layer < layers - 1:
                diag = diag + vert[layer, part, :]
            scale = 1.0 / diag
            cn[layer, part, :] = north * scale
            cs[layer, part, :] = south * scale
            cw[layer, part, :] = jnp.where(west_end, 0.0, west * scale)
            ce[layer, part, :] = jnp.where(east_end, 0.0, east * scale)
            if layer > 0:
                cu[layer, part, :] = vert[layer - 1, part, :] * scale
            if layer < layers - 1:
                cd[layer, part, :] = vert[layer, part, :] * scale
            first = rech_ref[layer, part, :] * scale
            base[layer, part, :] = first
            head_a[layer, PAD + r:PAD + r + CHUNK, :] = first

    old, new = head_a, head_b
    for sweep in range(PASSES - 1):
        for layer in range(layers):
            shift = shift_of(sweep * layers + layer)
            for r in range(0, rows, CHUNK):
                part = pl.ds(r, CHUNK)
                h = old[layer, PAD + r:PAD + r + CHUNK, :]
                beyond = pltpu.roll(halo[part, :], shift, 1)
                total = base[layer, part, :]
                total = total + cn[layer, part, :] * old[layer, PAD + r - 1:PAD + r + CHUNK - 1, :]
                total = total + cs[layer, part, :] * old[layer, PAD + r + 1:PAD + r + CHUNK + 1, :]
                total = total + cw[layer, part, :] * jnp.where(west_cut, beyond, pltpu.roll(h, 1, 1))
                total = total + ce[layer, part, :] * jnp.where(east_cut, beyond, pltpu.roll(h, columns - 1, 1))
                if layer > 0:
                    total = total + cu[layer, part, :] * old[layer - 1, PAD + r:PAD + r + CHUNK, :]
                if layer < layers - 1:
                    total = total + cd[layer, part, :] * old[layer + 1, PAD + r:PAD + r + CHUNK, :]
                new[layer, PAD + r:PAD + r + CHUNK, :] = total
        old, new = new, old

    stride = 2 * layers + 1
    pack_rows(
        lambda layer, start: old[layer, pl.ds(PAD + start, 8, stride=2), :],
        send_ref, layers, rows, stride,
    )
    lane = lax.broadcasted_iota(jnp.int32, (1, columns), 1)
    wells = jnp.zeros((1, columns), jnp.float32)
    for k in range(STEPS):
        cell = cells_ref[order_ref[k]]
        width = 2 * columns
        layer = cell // (rows * width)
        row = cell // width % rows
        column = cell % width
        line = old[layer, pl.ds(PAD + row, 1), :]
        moved = pltpu.roll(line, lax.rem(k - column % columns + columns, columns), 1)
        mine = jnp.logical_and(lane == k, column // columns == core)
        wells = wells + jnp.where(mine, moved, 0.0)
    block = jnp.broadcast_to(wells, (8, columns))
    for g in range(0, rows // 2, 8):
        send_ref[pl.ds(stride * g + stride - 1, 8, stride=stride), :] = block


def wells_kernel(recv_ref, wells_ref):
    members = 128
    stride = recv_ref.shape[0] // members
    wells_ref[...] = recv_ref[pl.ds(stride - 1, members, stride=stride), :].T[:STEPS]


def apply_map(recv_ref, mix, out_ref, stride):
    members = mix.shape[0]
    for layer in range(4):
        for r in range(2):
            x = recv_ref[pl.ds(2 * layer + r, members, stride=stride), :]
            out_ref[pl.ds(layer * 2 * members + r, members, stride=2), :] = x + lax.dot_general(
                mix, x, (((1,), (0,)), ((), ())), precision=HIGHEST, preferred_element_type=jnp.float32
            )


def update_kernel(order_ref, obs_ref, var_ref, recv_ref, own_ref, other_ref, out_ref, mix_ref):
    members = own_ref.shape[1]
    y = own_ref[...] + other_ref[...]
    step_id = lax.broadcasted_iota(jnp.int32, y.shape, 0)
    gains = jnp.zeros_like(y)
    weights_all = jnp.zeros_like(y)
    for k in range(STEPS):
        well = order_ref[k]
        row = y[k:k + 1]
        mean_value = jnp.sum(row, axis=1, keepdims=True) * (1.0 / members)
        spread = row - mean_value
        variance = jnp.full((1, 1), var_ref[well], jnp.float32)
        denom = jnp.sum(spread * spread, axis=1, keepdims=True) / (members - 1) + variance
        alpha = 1.0 / (1.0 + jnp.sqrt(variance / denom))
        weights = (obs_ref[well] - mean_value) - alpha * spread
        factor = 1.0 / ((members - 1) * denom)
        earlier = jnp.sum(weights_all * spread, axis=1, keepdims=True)
        gain = factor * (spread + jnp.sum(gains * earlier, axis=0, keepdims=True))
        y = y + (factor * jnp.sum(y * spread, axis=1, keepdims=True)) * weights
        gains = jnp.where(step_id == k, gain, gains)
        weights_all = jnp.where(step_id == k, weights, weights_all)
    mix = lax.dot_general(
        weights_all, gains, (((0,), (0,)), ((), ())), precision=HIGHEST,
        preferred_element_type=jnp.float32,
    )
    mix_ref[...] = mix
    apply_map(recv_ref, mix, out_ref, recv_ref.shape[0] // members)


def perm_kernel(recv_ref, mix_ref, out_ref):
    apply_map(recv_ref, mix_ref[...], out_ref, recv_ref.shape[0] // mix_ref.shape[0])


def call(kernel, out, in_specs, scratch=()):
    return pl.pallas_call(
        kernel, out_shape=out, in_specs=in_specs,
        out_specs=jax.tree.map(lambda _: VMEM, out),
        scratch_shapes=list(scratch), compiler_params=PARAMS,
    )


def f32(*shape):
    return jax.ShapeDtypeStruct(shape, jnp.float32)


def exchange(send, parts):
    rows = send.shape[0] // parts
    moved = lax.all_to_all(
        send.reshape(parts, rows, 1, send.shape[1]), "gx", split_axis=0, concat_axis=0, tiled=True
    )
    return moved.reshape(send.shape)


def body(log_perm, recharge, well_cells, observed, variances, well_order):
    layers, _, rows, columns = log_perm.shape
    parts = lax.axis_size("gx")
    core = lax.axis_index("gy").astype(jnp.int32).reshape(1)
    swap = [(0, 1), (1, 0)]
    perm = log_perm.reshape(layers, rows, columns)
    near, away = call(
        edges_kernel, (f32(2, layers, HALO, rows),) * 2, [SMEM, VMEM, VMEM]
    )(core, perm, recharge)
    far = lax.ppermute(away, "gy", swap)
    perm_send = call(pack_kernel, f32(parts * 8, columns), [VMEM])(perm)
    field = pltpu.VMEM((layers, rows, columns), jnp.float32)
    padded = pltpu.VMEM((layers, rows + 2 * PAD, columns), jnp.float32)
    head_send = call(
        jacobi_kernel, f32(parts * 9, columns), [SMEM] * 3 + [VMEM] * 4,
        [padded, padded] + [field] * 8 + [padded, padded, pltpu.VMEM((rows, columns), jnp.float32)],
    )(core, well_cells, well_order, perm, recharge, near, far)
    head_send, perm_send = lax.optimization_barrier((head_send, perm_send))
    head_recv = exchange(head_send, parts)
    perm_recv = exchange(perm_send, parts)
    own = call(wells_kernel, f32(STEPS, parts), [VMEM])(head_recv)
    other = lax.ppermute(own, "gy", swap)
    out = f32(layers * parts * 2, columns)
    post_head, mix = call(
        update_kernel, (out, f32(parts, parts)), [SMEM] * 3 + [VMEM] * 3
    )(well_order, observed, variances, head_recv, own, other)
    post_perm = call(perm_kernel, out, [VMEM, VMEM])(perm_recv, mix)
    shape = (layers, parts, 2, columns)
    return post_perm.reshape(shape), post_head.reshape(shape)


def solution(mesh):
    placed = (P(None, "gx", None, "gy"), P(None, None, "gy"), P(), P(), P(), P())
    return jax.shard_map(
        body,
        mesh=mesh,
        in_specs=placed,
        out_specs=(P(None, None, "gx", "gy"), P(None, None, "gx", "gy")),
        check_vma=False,
    )
```

time: 832 us -> 75 us (0.09)
  the two profiles are of different devices: /device:TPU:1 before, /device:TPU:2 now
where the time goes in v1:
time: 75 us; the launch traced here: 74.7 us
  blocking collectives  37.2 us (50%)
  waiting for transfers between devices  15.6 us (21%)
  Pallas kernels  11.9 us (16%)
  starting transfers between devices  6.89 us (9%)
  local copies, waits for them, and re-layouts  2.47 us (3%)
    all_to_all x1, blocking collectives, exchange(): lax.all_to_all(send.reshape(parts, rows, 1, send.shape[1]), 'gx', split_a...  37.2 us
    all_to_all x1, waiting for transfers between devices, exchange(): lax.all_to_all(send.reshape(parts, rows, 1, send.shape[1]), 'gx', split_a...  14.1 us
    all_to_all x1, starting transfers between devices, exchange(): lax.all_to_all(send.reshape(parts, rows, 1, send.shape[1]), 'gx', split_a...  6.81 us
    pallas_call x1, Pallas kernels, body(): call(jacobi_kernel, f32(parts * 9, columns), [SMEM] * 3 + [VMEM] * 4, [pa...  4.92 us
    pallas_call x1, Pallas kernels, body(): call(update_kernel, (out, f32(parts, parts)), [SMEM] * 3 + [VMEM] * 3)  3.64 us
    unnamed x14, local copies, waits for them, and re-layouts  2.47 us
  transfers between devices with their start and end apart: 3, of which 3 were waited for; matrix products, arithmetic and copies ran while one was open for 0% of the time, Pallas kernels for 6%

profile of v1, /device:TPU:2, one launch (start us, length us, event | category | flops | bytes accessed | tf_op | source)
XLA Modules:
  0.0 74.7 jit_solution(16459133089366451164)
XLA Ops:
  0.6 0.0 copy-start
  0.6 1.0 %copy-done = f32[4,1,256,128]{3,2,1,0:T(8,128)S(1)} copy-done((f32[4,1,256,128]{3,2,1,0:T(8,128)S(1)}, f32[4,1,256,128]{3,2,1,0:T(8,128)}, u32[]{:S(2)}) %copy-start) | copy-done | bytes 524312
  1.7 0.0 copy-start.1
  1.7 1.0 %copy-done.1 = f32[4,256,128]{2,1,0:T(8,128)S(1)} copy-done((f32[4,256,128]{2,1,0:T(8,128)S(1)}, f32[4,256,128]{2,1,0:T(8,128)}, u32[]{:S(2)}) %copy-start.1) | copy-done | bytes 524312
  2.7 0.9 %shard_map.77 = (f32[2,4,8,256]{3,2,1,0:T(8,128)S(1)}, f32[2,4,8,256]{3,2,1,0:T(8,128)S(1)}) custom-call(s32[1]{0:T(128)} %bitcast.core_ref, f32[4,256,128]{2,1,0:T(8,128)S(1)} %bitcast.12, f32[4,256,128]{2,1,0:T(8,128)S(1)} %copy-done.1), custom_call_target="tpu_custom_call" | custom-call | tf_op jit(solution)/shard_map/pallas_call | solution.py:301
  3.7 0.0 copy-start.2
  3.7 0.0 collective-permute-start
  3.7 0.9 %shard_map.79 = f32[1024,128]{1,0:T(8,128)} custom-call(f32[4,256,128]{2,1,0:T(8,128)S(1)} %bitcast.13), custom_call_target="tpu_custom_call" | custom-call | tf_op jit(solution)/shard_map/pallas_call | solution.py:305
  4.6 0.0 copy-start.3
  4.6 0.0 copy-start.4
  4.6 0.3 collective-permute-done.far_ref
  4.9 0.0 copy-done.2
  4.9 0.4 copy-done.3
  5.3 0.0 copy-done.4
  5.3 4.9 %shard_map.78 = f32[1152,128]{1,0:T(8,128)S(1)} custom-call(s32[1]{0:T(128)} %bitcast.core_ref, s32[32]{0:T(128)S(1)} %copy-done.4, s32[8]{0:T(128)S(1)} %copy-done.3, f32[4,256,128]{2,1,0:T(8,128)S(1)} %bitcast.14, f32[4,256,128]{2,1,0:T(8,128)S(1)} %copy-done.2, f32[2,4,8,256]{3,2,1,0:T(8,128)S(1)} %get-tuple-element.8.near_ref, ...), custom_call_target="tpu_custom_call" | custom-call | tf_op jit(solution)/shard_map/pallas_call | solution.py:308
  10.2 37.2 %all_to_all.10 = f32[128,9,1,128]{3,2,1,0:T(1,128)S(1)} all-to-all(f32[128,9,1,128]{3,2,1,0:T(1,128)S(1)} %bitcast.15), channel_id=1, replica_groups=mesh['gx'=128,'gy'=2] {'gx'}, dimensions={0} | all-to-all | bytes 1179648 | tf_op jit(solution)/shard_map/all_to_all | solution.py:289
  47.5 6.8 %all-to-all-start = ((f32[128,8,1,128]{3,1,2,0:T(8,128)}), f32[128,8,1,128]{3,1,2,0:T(8,128)S(1)}, u32[]{:S(2)}, u32[]{:S(2)}) async-start(f32[128,8,1,128]{3,1,2,0:T(8,128)} %bitcast.3), calls=%async_computation | async-start | bytes 1048576 | tf_op jit(solution)/shard_map/all_to_all | solution.py:289
  54.3 0.0 copy-start.5
  54.3 0.0 copy-start.6
  54.3 0.1 collective-permute-start.1
  54.4 1.2 %collective-permute-done.1.other_ref = f32[8,128]{1,0:T(8,128)S(1)} collective-permute-done((f32[8,128]{1,0:T(8,128)S(1)}, f32[8,128]{1,0:T(8,128)S(1)}, u32[]{:S(2)}, u32[]{:S(2)}) %collective-permute-start.1) | collective-permute-done | bytes 4128 | tf_op jit(solution)/shard_map/ppermute | solution.py:316
  55.6 0.0 copy-done.5
  55.6 0.0 copy-done.6
  55.6 3.6 %shard_map.81 = (f32[1024,128]{1,0:T(8,128)}, f32[128,128]{1,0:T(8,128)S(1)}) custom-call(s32[8]{0:T(128)S(1)} %copy-done.3, f32[32]{0:T(128)S(1)} %copy-done.5, f32[32]{0:T(128)S(1)} %copy-done.6, f32[1152,128]{1,0:T(8,128)S(1)} %bitcast.11, f32[8,128]{1,0:T(8,128)S(1)} %shard_map.80.own_ref, f32[8,128]{1,0:T(8,128)S(1)} %collective-permute-done.1.other_ref), custom_call_target="tpu_custom_call" | custom-call | tf_op jit(solution)/shard_map/pallas_call | solution.py:318
  59.2 14.1 %all-to-all-done = f32[128,8,1,128]{3,1,2,0:T(8,128)S(1)} async-done(((f32[128,8,1,128]{3,1,2,0:T(8,128)}), f32[128,8,1,128]{3,1,2,0:T(8,128)S(1)}, u32[]{:S(2)}, u32[]{:S(2)}) %all-to-all-start) | async-done | bytes 524320 | tf_op jit(solution)/shard_map/all_to_all | solution.py:289
  73.3 1.4 %shard_map.82 = f32[1024,128]{1,0:T(8,128)} custom-call(f32[1024,128]{1,0:T(8,128)S(1)} %bitcast.16, f32[128,128]{1,0:T(8,128)S(1)} %get-tuple-element.12.mix_ref), custom_call_target="tpu_custom_call" | custom-call | tf_op jit(solution)/shard_map/pallas_call | solution.py:321
  (1 shorter events, 0.0 us)
Async XLA Ops:
  0.6 1.0 %copy-start = (f32[4,1,256,128]{3,2,1,0:T(8,128)S(1)}, f32[4,1,256,128]{3,2,1,0:T(8,128)}, u32[]{:S(2)}) copy-start(f32[4,1,256,128]{3,2,1,0:T(8,128)} %param.6) | copy-start | bytes 1572868
  1.7 1.0 %copy-start.1 = (f32[4,256,128]{2,1,0:T(8,128)S(1)}, f32[4,256,128]{2,1,0:T(8,128)}, u32[]{:S(2)}) copy-start(f32[4,256,128]{2,1,0:T(8,128)} %rech_ref.3) | copy-start | bytes 1572868
  3.7 1.3 %copy-start.2 = (f32[4,256,128]{2,1,0:T(8,128)S(1)}, f32[4,256,128]{2,1,0:T(8,128)}, u32[]{:S(2)}) copy-start(f32[4,256,128]{2,1,0:T(8,128)} %rech_ref.3) | copy-start | bytes 1572868
  3.7 1.3 %collective-permute-start = (f32[2,4,8,256]{3,2,1,0:T(8,128)S(1)}, f32[2,4,8,256]{3,2,1,0:T(8,128)S(1)}, u32[]{:S(2)}, u32[]{:S(2)}) collective-permute-start(f32[2,4,8,256]{3,2,1,0:T(8,128)S(1)} %get-tuple-element.9), channel_id=1, source_target_pairs={{0,1},{1,0},{2,3},{3,2},{4,5},{5,4},{6,7},{7,6},{8,9},{9,8},{10,11... | collective-permute-start | bytes 196616 | tf_op jit(solution)/shard_map/ppermute | solution.py:304
  4.6 0.7 copy-start.3
  4.6 0.7 copy-start.4
  47.5 25.9 %all-to-all-start = ((f32[128,8,1,128]{3,1,2,0:T(8,128)}), f32[128,8,1,128]{3,1,2,0:T(8,128)S(1)}, u32[]{:S(2)}, u32[]{:S(2)}) async-start(f32[128,8,1,128]{3,1,2,0:T(8,128)} %bitcast.3), calls=%async_computation | async-start | bytes 1048576 | tf_op jit(solution)/shard_map/all_to_all | solution.py:289
  54.3 1.3 %copy-start.5 = (f32[32]{0:T(128)S(1)}, f32[32]{0:T(128)}, u32[]{:S(2)}) copy-start(f32[32]{0:T(128)} %obs_ref.1) | copy-start | bytes 388
  54.3 1.3 %copy-start.6 = (f32[32]{0:T(128)S(1)}, f32[32]{0:T(128)}, u32[]{:S(2)}) copy-start(f32[32]{0:T(128)} %var_ref.1) | copy-start | bytes 388
  54.3 1.2 %collective-permute-start.1 = (f32[8,128]{1,0:T(8,128)S(1)}, f32[8,128]{1,0:T(8,128)S(1)}, u32[]{:S(2)}, u32[]{:S(2)}) collective-permute-start(f32[8,128]{1,0:T(8,128)S(1)} %shard_map.80.own_ref), channel_id=1, source_target_pairs={{0,1},{1,0},{2,3},{3,2},{4,5},{5,4},{6,7},{7,6},{8,9},{9,8},{10,11... | collective-permute-start | bytes 12296 | tf_op jit(solution)/shard_map/ppermute | solution.py:316

commit v2 on v0

v2 whole, which is shorter than its diff:
```python
import functools

import jax
import jax.numpy as jnp
from jax import lax
from jax.experimental import pallas as pl
from jax.experimental.pallas import tpu as pltpu
from jax.sharding import PartitionSpec as P

PASSES = 8
STEPS = 8
VERT = 0.1
LEAK = 0.1
PAD = 8
CHUNK = 32
HIGHEST = lax.Precision.HIGHEST

VMEM = pl.BlockSpec(memory_space=pltpu.VMEM)
SMEM = pl.BlockSpec(memory_space=pltpu.SMEM)
HBM = pl.BlockSpec(memory_space=pltpu.HBM)
PARAMS = pltpu.CompilerParams(vmem_limit_bytes=48 * 1024 * 1024)


def stage_kernel(perm_any, rech_any, perm_ref, rech_ref, sems):
    copies = []
    for which, (source, target) in enumerate(((perm_any, perm_ref), (rech_any, rech_ref))):
        for layer in range(source.shape[0]):
            copies.append(pltpu.make_async_copy(source.at[layer], target.at[layer], sems.at[which, layer]))
    for copy in copies:
        copy.start()
    for copy in copies:
        copy.wait()


def harmonic_inv(a, b):
    return 2.0 / (a + b)


def pack_rows(load, send_ref, layers, rows, stride):
    for half in range(2):
        for layer in range(layers):
            for r in range(2):
                row = 2 * layers * half + 2 * layer + r
                for g in range(0, rows // 2, 8):
                    send_ref[pl.ds(stride * g + row, 8, stride=stride), :] = load(half, layer, 2 * g + r)


def jacobi(perm, rech, send_ref, inv, rowt, vert, cn, cs, cw, ce, cu, cd, base, head_a, head_b):
    layers, rows, columns = perm[0].shape
    lane = lax.broadcasted_iota(jnp.int32, (CHUNK, columns), 1)
    west_end, east_end = lane == 0, lane == columns - 1
    ones = jnp.ones((PAD, columns), jnp.float32)
    zeros = jnp.zeros((PAD, columns), jnp.float32)
    for half in range(2):
        for layer in range(layers):
            inv[half, layer, 0:PAD, :] = ones
            inv[half, layer, PAD + rows:2 * PAD + rows, :] = ones
            for ref in (head_a, head_b):
                ref[half, layer, 0:PAD, :] = zeros
                ref[half, layer, PAD + rows:2 * PAD + rows, :] = zeros

    def chunks(work):
        for r in range(0, rows, CHUNK):
            work(r)

    def invert(r):
        for half in range(2):
            for layer in range(layers):
                inv[half, layer, pl.ds(PAD + r, CHUNK), :] = jnp.exp(-perm[half][layer, pl.ds(r, CHUNK), :])

    chunks(invert)
    for half in range(2):
        for layer in range(layers):
            rowt[half, layer, 0:PAD, :] = harmonic_inv(inv[half, layer, 0:PAD, :], inv[half, layer, 1:PAD + 1, :])

    def down(r):
        for half in range(2):
            for layer in range(layers):
                rowt[half, layer, pl.ds(PAD + r, CHUNK), :] = harmonic_inv(
                    inv[half, layer, pl.ds(PAD + r, CHUNK), :], inv[half, layer, pl.ds(PAD + r + 1, CHUNK), :]
                )

    chunks(down)

    def weigh(r):
        part = pl.ds(r, CHUNK)
        for layer in range(layers):
            left = inv[0, layer, pl.ds(PAD + r, CHUNK), :]
            right = inv[1, layer, pl.ds(PAD + r, CHUNK), :]
            left_e, right_e = pltpu.roll(left, columns - 1, 1), pltpu.roll(right, columns - 1, 1)
            east = [
                harmonic_inv(left, jnp.where(east_end, right_e, left_e)),
                harmonic_inv(right, jnp.where(east_end, 1.0, right_e)),
            ]
            left_w, right_w = pltpu.roll(east[0], 1, 1), pltpu.roll(east[1], 1, 1)
            west = [
                jnp.where(west_end, harmonic_inv(left, 1.0), left_w),
                jnp.where(west_end, left_w, right_w),
            ]
            for half, here in enumerate((left, right)):
                north = rowt[half, layer, pl.ds(PAD + r - 1, CHUNK), :]
                south = rowt[half, layer, pl.ds(PAD + r, CHUNK), :]
                diag = LEAK + north + south + west[half] + east[half]
                if layer > 0:
                    upper = vert[half, layer - 1, part, :]
                    diag = diag + upper
                if layer < layers - 1:
                    lower = VERT * harmonic_inv(here, inv[half, layer + 1, pl.ds(PAD + r, CHUNK), :])
                    vert[half, layer, part, :] = lower
                    diag = diag + lower
                scale = 1.0 / diag
                cn[half, layer, part, :] = north * scale
                cs[half, layer, part, :] = south * scale
                w, e = west[half] * scale, east[half] * scale
                cw[half, layer, part, :] = jnp.where(west_end, 0.0, w) if half == 0 else w
                ce[half, layer, part, :] = jnp.where(east_end, 0.0, e) if half == 1 else e
                if layer > 0:
                    cu[half, layer, part, :] = upper * scale
                if layer < layers - 1:
                    cd[half, layer, part, :] = lower * scale
                first = rech[half][layer, part, :] * scale
                base[half, layer, part, :] = first
                head_a[half, layer, pl.ds(PAD + r, CHUNK), :] = first

    chunks(weigh)

    def relax(old, new):
        def work(r):
            part = pl.ds(r, CHUNK)
            here = [[old[half, layer, pl.ds(PAD + r, CHUNK), :] for half in range(2)] for layer in range(layers)]
            for layer in range(layers):
                left, right = here[layer]
                left_w, right_w = pltpu.roll(left, 1, 1), pltpu.roll(right, 1, 1)
                left_e, right_e = pltpu.roll(left, columns - 1, 1), pltpu.roll(right, columns - 1, 1)
                west = [left_w, jnp.where(west_end, left_w, right_w)]
                east = [jnp.where(east_end, right_e, left_e), right_e]
                for half in range(2):
                    one = cn[half, layer, part, :] * old[half, layer, pl.ds(PAD + r - 1, CHUNK), :]
                    two = cs[half, layer, part, :] * old[half, layer, pl.ds(PAD + r + 1, CHUNK), :]
                    one = one + cw[half, layer, part, :] * west[half]
                    two = two + ce[half, layer, part, :] * east[half]
                    if layer > 0:
                        one = one + cu[half, layer, part, :] * here[layer - 1][half]
                    if layer < layers - 1:
                        two = two + cd[half, layer, part, :] * here[layer + 1][half]
                    new[half, layer, pl.ds(PAD + r, CHUNK), :] = base[half, layer, part, :] + one + two

        chunks(work)

    def two_passes(_, carry):
        relax(head_a, head_b)
        relax(head_b, head_a)
        return carry

    lax.fori_loop(0, (PASSES - 2) // 2, two_passes, 0)
    relax(head_a, head_b)
    last = head_b

    stride = send_ref.shape[0] * 2 // rows
    pack_rows(
        lambda half, layer, start: last[half, layer, pl.ds(PAD + start, 8, stride=2), :],
        send_ref, layers, rows, stride,
    )
    return last


def put_wells(last, cells_ref, order_ref, send_ref):
    rows, columns = last.shape[2] - 2 * PAD, last.shape[3]
    stride = send_ref.shape[0] * 2 // rows
    spot = lax.broadcasted_iota(jnp.int32, (1, columns), 1)
    wells = jnp.zeros((1, columns), jnp.float32)
    for k in range(STEPS):
        cell = cells_ref[order_ref[k]]
        width = 2 * columns
        line = last[cell % width // columns, cell // (rows * width), pl.ds(PAD + cell // width % rows, 1), :]
        moved = pltpu.roll(line, lax.rem(k - cell % columns + columns, columns), 1)
        wells = jnp.where(spot == k, moved, wells)
    block = jnp.broadcast_to(wells, (8, columns))
    for g in range(0, rows // 2, 8):
        send_ref[pl.ds(stride * g + stride - 1, 8, stride=stride), :] = block


def produce_kernel(
    core_ref, cells_any, order_any, perm_ref, rech_ref, perm_far, rech_far, send_ref,
    cells_ref, order_ref, sems, *scratch,
):
    layers, rows, columns = perm_ref.shape

    @pl.when(core_ref[0] == 0)
    def _():
        copies = [
            pltpu.make_async_copy(cells_any, cells_ref, sems.at[0]),
            pltpu.make_async_copy(order_any, order_ref, sems.at[1]),
        ]
        for copy in copies:
            copy.start()
        last = jacobi((perm_ref, perm_far), (rech_ref, rech_far), send_ref, *scratch)
        for copy in copies:
            copy.wait()
        put_wells(last, cells_ref, order_ref, send_ref)

    @pl.when(core_ref[0] == 1)
    def _():
        stride = send_ref.shape[0] * 2 // rows
        both = (perm_far, perm_ref)
        pack_rows(
            lambda half, layer, start: both[half][layer, pl.ds(start, 8, stride=2), :],
            send_ref, layers, rows, stride,
        )
        blank = jnp.zeros((8, columns), jnp.float32)
        for g in range(0, rows // 2, 8):
            send_ref[pl.ds(stride * g + stride - 1, 8, stride=stride), :] = blank


def split_kernel(core_ref, recv_ref, wells_ref, give_ref):
    members, stride = 128, recv_ref.shape[0] // 128
    wells_ref[...] = recv_ref[pl.ds(stride - 1, members, stride=stride), :].T[:STEPS]
    for core in range(2):
        @pl.when(core_ref[0] == core)
        def _():
            for j in range(8):
                give_ref[pl.ds(members * j, members), :] = recv_ref[
                    pl.ds(8 * (1 - core) + j, members, stride=stride), :
                ]


def steps_kernel(core_ref, order_ref, obs_ref, var_ref, own_ref, other_ref, mix_ref):
    members = own_ref.shape[1]
    y = jnp.where(core_ref[0] == 0, own_ref[...], other_ref[...])
    step_id = lax.broadcasted_iota(jnp.int32, y.shape, 0)
    means = jnp.sum(y, axis=1, keepdims=True) * (1.0 / members)
    spreads = y - means
    gains = jnp.zeros_like(y)
    weights_all = jnp.zeros_like(y)
    for k in range(STEPS):
        well = order_ref[k]
        spread = spreads[k:k + 1]
        variance = jnp.full((1, 1), var_ref[well], jnp.float32)
        products = jnp.sum(spreads * spread, axis=1, keepdims=True)
        denom = products[k:k + 1] / (members - 1) + variance
        alpha = 1.0 / (1.0 + jnp.sqrt(variance / denom))
        shift = obs_ref[well] - means[k:k + 1]
        weights = shift - alpha * spread
        factor = 1.0 / ((members - 1) * denom)
        earlier = jnp.sum(weights_all * spread, axis=1, keepdims=True)
        gain = factor * (spread + jnp.sum(gains * earlier, axis=0, keepdims=True))
        rate = factor * products
        means = means + rate * shift
        spreads = spreads - (rate * alpha) * spread
        gains = jnp.where(step_id == k, gain, gains)
        weights_all = jnp.where(step_id == k, weights, weights_all)
    mix_ref[...] = lax.dot_general(
        weights_all, gains, (((0,), (0,)), ((), ())), precision=HIGHEST,
        preferred_element_type=jnp.float32,
    )


def apply_kernel(core_ref, recv_ref, got_ref, mix_ref, perm_ref, head_ref):
    members, stride = 128, recv_ref.shape[0] // 128
    layer = pl.program_id(0)
    mix = mix_ref[...]

    def put(out_ref, r, x):
        out_ref[pl.ds(r, members, stride=2), :] = x + lax.dot_general(
            mix, x, (((1,), (0,)), ((), ())), precision=HIGHEST, preferred_element_type=jnp.float32
        )

    for core, kept, taken in ((0, head_ref, perm_ref), (1, perm_ref, head_ref)):
        @pl.when(core_ref[0] == core)
        def _():
            for r in range(2):
                row = 2 * layer + r
                put(kept, r, recv_ref[pl.ds(8 * core + row, members, stride=stride), :])
                put(taken, r, got_ref[pl.ds(pl.multiple_of(members * row, members), members), :])


def call(kernel, out, in_specs, scratch=()):
    return pl.pallas_call(
        kernel, out_shape=out, in_specs=in_specs,
        out_specs=jax.tree.map(lambda _: VMEM, out),
        scratch_shapes=list(scratch), compiler_params=PARAMS,
    )


def f32(*shape):
    return jax.ShapeDtypeStruct(shape, jnp.float32)


def produce(core, cells, order, perm, rech, perm_far, rech_far):
    layers, rows, columns = perm.shape
    field = pltpu.VMEM((2, layers, rows, columns), jnp.float32)
    padded = pltpu.VMEM((2, layers, rows + 2 * PAD, columns), jnp.float32)
    return call(
        produce_kernel, f32(rows // 2 * (4 * layers + 1), columns), [SMEM, HBM, HBM] + [VMEM] * 4,
        [pltpu.SMEM(cells.shape, jnp.int32), pltpu.SMEM(order.shape, jnp.int32), pltpu.SemaphoreType.DMA((2,))]
        + [padded, padded] + [field] * 8 + [padded, padded],
    )(core, cells, order, perm, rech, perm_far, rech_far)


def body(log_perm, recharge, well_cells, observed, variances, well_order):
    layers, _, rows, columns = log_perm.shape
    parts = lax.axis_size("gx")
    core = lax.axis_index("gy").astype(jnp.int32).reshape(1)
    swap = [(0, 1), (1, 0)]
    perm = log_perm.reshape(layers, rows, columns)
    perm_far = lax.ppermute(perm, "gy", swap)
    rech_far = lax.ppermute(recharge, "gy", swap)
    perm = pltpu.with_memory_space_constraint(perm, pltpu.HBM)
    recharge = pltpu.with_memory_space_constraint(recharge, pltpu.HBM)
    well_cells = pltpu.with_memory_space_constraint(well_cells, pltpu.HBM)
    well_order_any = pltpu.with_memory_space_constraint(well_order, pltpu.HBM)
    perm, recharge = call(
        stage_kernel, (f32(*perm.shape), f32(*recharge.shape)), [HBM, HBM], [pltpu.SemaphoreType.DMA((2, layers))]
    )(perm, recharge)
    send = produce(core, well_cells, well_order_any, perm, recharge, perm_far, rech_far)
    recv = lax.all_to_all(
        send.reshape(parts, -1, 1, columns), "gx", split_axis=0, concat_axis=0, tiled=True
    ).reshape(send.shape)
    own, give = call(
        split_kernel, (f32(STEPS, parts), f32(parts * 2 * layers, columns)), [SMEM, VMEM]
    )(core, recv)
    other = lax.ppermute(own, "gy", swap)
    other, give = lax.optimization_barrier((other, give))
    got = lax.ppermute(give, "gy", swap)
    mix = call(
        steps_kernel, f32(parts, parts), [SMEM] * 4 + [VMEM] * 2
    )(core, well_order, observed, variances, own, other)
    block = pl.BlockSpec((2 * parts, columns), lambda layer: (layer, 0))
    out = f32(layers * parts * 2, columns)
    post_perm, post_head = pl.pallas_call(
        apply_kernel, out_shape=(out, out), grid=(layers,),
        in_specs=[SMEM, VMEM, VMEM, VMEM], out_specs=(block, block), compiler_params=PARAMS,
    )(core, recv, got, mix)
    shape = (layers, parts, 2, columns)
    return post_perm.reshape(shape), post_head.reshape(shape)


def solution(mesh):
    placed = (P(None, "gx", None, "gy"), P(None, None, "gy"), P(), P(), P(), P())
    return jax.shard_map(
        body,
        mesh=mesh,
        in_specs=placed,
        out_specs=(P(None, None, "gx", "gy"), P(None, None, "gx", "gy")),
        check_vma=False,
    )
```

time: 832 us -> 59.6 us (0.07)
  blocking collectives: 591 us -> 37.3 us
  loops' own time: 64.6 us -> 0 us
  starting transfers between devices: 69.6 us -> 13.6 us
  other arithmetic: 37.1 us -> 0 us
  local copies, waits for them, and re-layouts: 29.4 us -> 0.01 us
  waiting for transfers between devices: 27.9 us -> 1.86 us
  matrix products: 8.36 us -> 0 us
    psum x8 -> x0, blocking collectives: 591 us -> none  [spread_2(): return lax.psum(jnp.where(mine, x, jnp.zeros_like(x)), axis)]
    another operation x1 -> x0, loops' own time: 64.6 us -> none  [body(): lax.fori_loop(0, STEPS, step_single, (perm_rows, head_rows))]
    all_to_all x0 -> x1, blocking collectives: none -> 37.3 us  [body(): lax.all_to_all(send.reshape(parts, -1, 1, columns), 'gx', split_axis=0, c...]
    ppermute x18 -> x4, starting transfers between devices: 42 us -> 13.6 us  [the longest x1 9.86 us: body(): other = lax.ppermute(own, 'gy', swap)]
    all_to_all x2 -> x0, starting transfers between devices: 27.7 us -> none  [the longest x1 14.2 us: body(): lax.all_to_all(log_perm, 'gx', split_axis=2, concat_axis=1, tiled=True)]
    dynamic_slice x32 -> x0, local copies, waits for them, and re-layouts: 18.8 us -> none  [the longest x8 4.71 us: step_single(): observed[well]]
    all_to_all x2 -> x0, waiting for transfers between devices: 18.3 us -> none  [the longest x1 18.3 us: body(): lax.all_to_all(head, 'gx', split_axis=2, concat_axis=1, tiled=True)]
    div x8 -> x0, other arithmetic: 14.2 us -> none  [relax(): return (source + total) / diagonal]
  transfers between devices with their start and end apart: 20 -> 4, of which waited for: 9 -> 3; matrix products, arithmetic and copies ran while one was open for 4% -> 0% of each run, Pallas kernels for 0% -> 5%
where the time goes in v2:
time: 59.6 us; the launch traced here: 59.4 us
  blocking collectives  37.3 us (63%)
  starting transfers between devices  13.6 us (23%)
  Pallas kernels  5.91 us (10%)
  waiting for transfers between devices  1.86 us (3%)
  between operations  0.68 us (1%)
    all_to_all x1, blocking collectives, body(): lax.all_to_all(send.reshape(parts, -1, 1, columns), 'gx', split_axis=0, c...  37.3 us
    ppermute x1, starting transfers between devices, body(): other = lax.ppermute(own, 'gy', swap)  9.86 us
    ppermute x1, starting transfers between devices, body(): perm_far = lax.ppermute(perm, 'gy', swap)  3.33 us
    pallas_call x1, Pallas kernels, body(): pl.pallas_call(apply_kernel, out_shape=(out, out), grid=(layers,), in_spe...  2.62 us
    pallas_call x1, Pallas kernels, body(): call(steps_kernel, f32(parts, parts), [SMEM] * 4 + [VMEM] * 2)  1.72 us
    pallas_call x1, Pallas kernels, body(): call(stage_kernel, (f32(*perm.shape), f32(*recharge.shape)), [HBM, HBM],...  1.35 us
  transfers between devices with their start and end apart: 4, of which 3 were waited for; matrix products, arithmetic and copies ran while one was open for 0% of the time, Pallas kernels for 5%

profile of v2, /device:TPU:1, one launch (start us, length us, event | category | flops | bytes accessed | tf_op | source)
XLA Modules:
  0.0 59.4 jit_solution(16961691402163914927)
XLA Ops:
  0.6 3.3 %collective-permute-start = (f32[4,256,128]{2,1,0:T(8,128)}, f32[4,256,128]{2,1,0:T(8,128)S(1)}, u32[]{:S(2)}, u32[]{:S(2)}) collective-permute-start(f32[4,256,128]{2,1,0:T(8,128)} %bitcast.9), channel_id=1, source_target_pairs={{0,1},{1,0},{2,3},{3,2},{4,5},{5,4},{6,7},{7,6},{8,9},{9,8},{10,11... | collective-permute-start | bytes 1572872 | tf_op jit(solution)/shard_map/ppermute | solution.py:306
  4.0 0.1 collective-permute-start.1
  4.1 1.3 %shard_map.77 = (f32[4,256,128]{2,1,0:T(8,128)S(1)}, f32[4,256,128]{2,1,0:T(8,128)S(1)}) custom-call(f32[4,256,128]{2,1,0:T(8,128)} %bitcast.10, f32[4,256,128]{2,1,0:T(8,128)} %rech_any.1), custom_call_target="tpu_custom_call" | custom-call | tf_op jit(solution)/shard_map/pallas_call | solution.py:312
  5.4 0.3 collective-permute-done.perm_far
  5.7 0.7 %collective-permute-done.1.rech_far = f32[4,256,128]{2,1,0:T(8,128)S(1)} collective-permute-done((f32[4,256,128]{2,1,0:T(8,128)}, f32[4,256,128]{2,1,0:T(8,128)S(1)}, u32[]{:S(2)}, u32[]{:S(2)}) %collective-permute-start.1) | collective-permute-done | bytes 524320 | tf_op jit(solution)/shard_map/ppermute | solution.py:307
  6.5 0.1 shard_map.78
  6.6 37.3 %all_to_all.5 = f32[128,17,1,128]{3,2,1,0:T(1,128)S(1)} all-to-all(f32[128,17,1,128]{3,2,1,0:T(1,128)S(1)} %bitcast.8), channel_id=1, replica_groups=mesh['gx'=128,'gy'=2] {'gx'}, dimensions={0} | all-to-all | bytes 2228224 | tf_op jit(solution)/shard_map/all_to_all | solution.py:316
  43.9 0.0 copy-start
  43.9 0.0 copy-start.1
  43.9 0.0 copy-start.2
  43.9 0.1 shard_map.79
  44.0 9.9 %collective-permute-start.2 = (f32[8,128]{1,0:T(8,128)S(1)}, f32[8,128]{1,0:T(8,128)S(1)}, u32[]{:S(2)}, u32[]{:S(2)}) collective-permute-start(f32[8,128]{1,0:T(8,128)S(1)} %get-tuple-element.12.own_ref), channel_id=1, source_target_pairs={{0,1},{1,0},{2,3},{3,2},{4,5},{5,4},{6,7},{7,6},{8,9},{9,8},{10,11... | collective-permute-start | bytes 12296 | tf_op jit(solution)/shard_map/ppermute | solution.py:322
  53.9 0.8 %collective-permute-done.2.other_ref = f32[8,128]{1,0:T(8,128)S(1)} collective-permute-done((f32[8,128]{1,0:T(8,128)S(1)}, f32[8,128]{1,0:T(8,128)S(1)}, u32[]{:S(2)}, u32[]{:S(2)}) %collective-permute-start.2) | collective-permute-done | bytes 4128 | tf_op jit(solution)/shard_map/ppermute | solution.py:322
  54.7 0.3 collective-permute-start.3
  55.0 0.0 copy-done
  55.0 0.0 copy-done.1
  55.1 0.0 copy-done.2
  55.1 1.7 %shard_map.80.mix_ref = f32[128,128]{1,0:T(8,128)S(1)} custom-call(s32[1]{0:T(128)} %bitcast.core_ref, s32[8]{0:T(128)S(1)} %copy-done, f32[32]{0:T(128)S(1)} %copy-done.1, f32[32]{0:T(128)S(1)} %copy-done.2, f32[8,128]{1,0:T(8,128)S(1)} %get-tuple-element.12.own_ref, f32[8,128]{1,0:T(8,128)S(1)} %collective-permute-done.2.other_ref), custom_call_target="tpu_custom_call" | custom-call | tf_op jit(solution)/shard_map/pallas_call | solution.py:325
  56.8 0.0 collective-permute-done.3.got_ref
  56.8 2.6 %shard_map.81 = (f32[1024,128]{1,0:T(8,128)}, f32[1024,128]{1,0:T(8,128)}) custom-call(s32[1]{0:T(128)} %bitcast.core_ref, f32[2176,128]{1,0:T(8,128)S(1)} %bitcast.7, f32[1024,128]{1,0:T(8,128)S(1)} %collective-permute-done.3.got_ref, f32[128,128]{1,0:T(8,128)S(1)} %shard_map.80.mix_ref), custom_call_target="tpu_custom_call" | custom-call | tf_op jit(solution)/shard_map/pallas_call | solution.py:330
Async XLA Ops:
  0.6 5.1 %collective-permute-start = (f32[4,256,128]{2,1,0:T(8,128)}, f32[4,256,128]{2,1,0:T(8,128)S(1)}, u32[]{:S(2)}, u32[]{:S(2)}) collective-permute-start(f32[4,256,128]{2,1,0:T(8,128)} %bitcast.9), channel_id=1, source_target_pairs={{0,1},{1,0},{2,3},{3,2},{4,5},{5,4},{6,7},{7,6},{8,9},{9,8},{10,11... | collective-permute-start | bytes 1572872 | tf_op jit(solution)/shard_map/ppermute | solution.py:306
  4.0 2.5 %collective-permute-start.1 = (f32[4,256,128]{2,1,0:T(8,128)}, f32[4,256,128]{2,1,0:T(8,128)S(1)}, u32[]{:S(2)}, u32[]{:S(2)}) collective-permute-start(f32[4,256,128]{2,1,0:T(8,128)} %rech_any.1), channel_id=1, source_target_pairs={{0,1},{1,0},{2,3},{3,2},{4,5},{5,4},{6,7},{7,6},{8,9},{9,8},{10,11... | collective-permute-start | bytes 1572872 | tf_op jit(solution)/shard_map/ppermute | solution.py:307
  43.9 11.1 %copy-start = (s32[8]{0:T(128)S(1)}, s32[8]{0:T(128)}, u32[]{:S(2)}) copy-start(s32[8]{0:T(128)} %order_ref.1) | copy-start | bytes 100
  43.9 11.1 %copy-start.1 = (f32[32]{0:T(128)S(1)}, f32[32]{0:T(128)}, u32[]{:S(2)}) copy-start(f32[32]{0:T(128)} %obs_ref.1) | copy-start | bytes 388
  43.9 11.1 %copy-start.2 = (f32[32]{0:T(128)S(1)}, f32[32]{0:T(128)}, u32[]{:S(2)}) copy-start(f32[32]{0:T(128)} %var_ref.1) | copy-start | bytes 388
  44.0 10.7 %collective-permute-start.2 = (f32[8,128]{1,0:T(8,128)S(1)}, f32[8,128]{1,0:T(8,128)S(1)}, u32[]{:S(2)}, u32[]{:S(2)}) collective-permute-start(f32[8,128]{1,0:T(8,128)S(1)} %get-tuple-element.12.own_ref), channel_id=1, source_target_pairs={{0,1},{1,0},{2,3},{3,2},{4,5},{5,4},{6,7},{7,6},{8,9},{9,8},{10,11... | collective-permute-start | bytes 12296 | tf_op jit(solution)/shard_map/ppermute | solution.py:322
  54.7 2.1 %collective-permute-start.3 = (f32[1024,128]{1,0:T(8,128)S(1)}, f32[1024,128]{1,0:T(8,128)S(1)}, u32[]{:S(2)}, u32[]{:S(2)}) collective-permute-start(f32[1024,128]{1,0:T(8,128)S(1)} %get-tuple-element.14), channel_id=1, source_target_pairs={{0,1},{1,0},{2,3},{3,2},{4,5},{5,4},{6,7},{7,6},{8,9},{9,8},{10,11... | collective-permute-start | bytes 1572872 | tf_op jit(solution)/shard_map/ppermute | solution.py:324

commit v3 on v2

--- a/solution.py
+++ b/solution.py
@@ -21,13 +21,28 @@
 PARAMS = pltpu.CompilerParams(vmem_limit_bytes=48 * 1024 * 1024)
 
 
-def stage_kernel(perm_any, rech_any, perm_ref, rech_ref, sems):
+def stage_kernel(
+    perm_any, rech_any, order_any, obs_any, var_any, perm_ref, rech_ref, known_ref,
+    order_ref, obs_ref, var_ref, sems, small_sems,
+):
+    small = [
+        pltpu.make_async_copy(source, target, small_sems.at[which])
+        for which, (source, target) in enumerate(
+            ((order_any, order_ref), (obs_any, obs_ref), (var_any, var_ref))
+        )
+    ]
     copies = []
     for which, (source, target) in enumerate(((perm_any, perm_ref), (rech_any, rech_ref))):
         for layer in range(source.shape[0]):
             copies.append(pltpu.make_async_copy(source.at[layer], target.at[layer], sems.at[which, layer]))
-    for copy in copies:
+    for copy in small + copies:
         copy.start()
+    for copy in small:
+        copy.wait()
+    for k in range(STEPS):
+        well = order_ref[k]
+        known_ref[pl.ds(k, 1), :] = jnp.full((1, known_ref.shape[1]), obs_ref[well], jnp.float32)
+        known_ref[pl.ds(STEPS + k, 1), :] = jnp.full((1, known_ref.shape[1]), var_ref[well], jnp.float32)
     for copy in copies:
         copy.wait()
 
@@ -212,34 +227,34 @@
             send_ref[pl.ds(stride * g + stride - 1, 8, stride=stride), :] = blank
 
 
-def split_kernel(core_ref, recv_ref, wells_ref, give_ref):
+def wells_kernel(recv_ref, wells_ref):
     members, stride = 128, recv_ref.shape[0] // 128
     wells_ref[...] = recv_ref[pl.ds(stride - 1, members, stride=stride), :].T[:STEPS]
-    for core in range(2):
-        @pl.when(core_ref[0] == core)
-        def _():
-            for j in range(8):
-                give_ref[pl.ds(members * j, members), :] = recv_ref[
-                    pl.ds(8 * (1 - core) + j, members, stride=stride), :
-                ]
-
-
-def steps_kernel(core_ref, order_ref, obs_ref, var_ref, own_ref, other_ref, mix_ref):
+
+
+def give_kernel(core_ref, recv_ref, after_ref, give_ref):
+    members, stride = 128, recv_ref.shape[0] // 128
+    for j in range(8):
+        give_ref[pl.ds(members * j, members), :] = recv_ref[
+            pl.ds(8 * (1 - core_ref[0]) + j, members, stride=stride), :
+        ]
+
+
+def steps_kernel(known_ref, own_ref, mix_ref):
     members = own_ref.shape[1]
-    y = jnp.where(core_ref[0] == 0, own_ref[...], other_ref[...])
+    y = own_ref[...]
     step_id = lax.broadcasted_iota(jnp.int32, y.shape, 0)
     means = jnp.sum(y, axis=1, keepdims=True) * (1.0 / members)
     spreads = y - means
     gains = jnp.zeros_like(y)
     weights_all = jnp.zeros_like(y)
     for k in range(STEPS):
-        well = order_ref[k]
         spread = spreads[k:k + 1]
-        variance = jnp.full((1, 1), var_ref[well], jnp.float32)
+        variance = known_ref[STEPS + k:STEPS + k + 1, :]
         products = jnp.sum(spreads * spread, axis=1, keepdims=True)
         denom = products[k:k + 1] / (members - 1) + variance
         alpha = 1.0 / (1.0 + jnp.sqrt(variance / denom))
-        shift = obs_ref[well] - means[k:k + 1]
+        shift = known_ref[k:k + 1, :] - means[k:k + 1]
         weights = shift - alpha * spread
         factor = 1.0 / ((members - 1) * denom)
         earlier = jnp.sum(weights_all * spread, axis=1, keepdims=True)
@@ -255,23 +270,53 @@
     )
 
 
-def apply_kernel(core_ref, recv_ref, got_ref, mix_ref, perm_ref, head_ref):
+def apply_kernel(core_ref, recv_ref, got_ref, own_mix_ref, other_mix_ref, perm_out, head_out, kept, taken, sems):
     members, stride = 128, recv_ref.shape[0] // 128
-    layer = pl.program_id(0)
-    mix = mix_ref[...]
-
-    def put(out_ref, r, x):
-        out_ref[pl.ds(r, members, stride=2), :] = x + lax.dot_general(
-            mix, x, (((1,), (0,)), ((), ())), precision=HIGHEST, preferred_element_type=jnp.float32
+    layers = kept.shape[0]
+    core = core_ref[0]
+    mix = jnp.where(core == 0, own_mix_ref[...], other_mix_ref[...])
+    mix_high, mix_low = split_bf16(mix)
+    mixes = jnp.concatenate([mix_high, mix_high, mix_low], 1)
+
+    def copies(own_out, got_out, layer):
+        return [
+            pltpu.make_async_copy(kept.at[layer], own_out.at[layer], sems.at[0, layer]),
+            pltpu.make_async_copy(taken.at[layer], got_out.at[layer], sems.at[1, layer]),
+        ]
+
+    for layer in range(layers):
+        x = jnp.concatenate(
+            [recv_ref[pl.ds(8 * core + 2 * layer + r, members, stride=stride), :] for r in range(2)]
+            + [got_ref[pl.ds(members * (2 * layer + r), members), :] for r in range(2)], 1
         )
-
-    for core, kept, taken in ((0, head_ref, perm_ref), (1, perm_ref, head_ref)):
-        @pl.when(core_ref[0] == core)
+        high, low = split_bf16(x)
+        x = x + jnp.dot(
+            mixes, jnp.concatenate([high, low, high], 0), preferred_element_type=jnp.float32
+        )
+        columns = x.shape[1] // 4
+        for place, ref in enumerate((kept, taken)):
+            for r in range(2):
+                at = (2 * place + r) * columns
+                ref[layer, pl.ds(r, members, stride=2), :] = x[:, at:at + columns]
+
+        @pl.when(core == 0)
         def _():
-            for r in range(2):
-                row = 2 * layer + r
-                put(kept, r, recv_ref[pl.ds(8 * core + row, members, stride=stride), :])
-                put(taken, r, got_ref[pl.ds(pl.multiple_of(members * row, members), members), :])
+            for copy in copies(head_out, perm_out, layer):
+                copy.start()
+
+        @pl.when(core == 1)
+        def _():
+            for copy in copies(perm_out, head_out, layer):
+                copy.start()
+
+    for layer in range(layers):
+        for copy in copies(head_out, perm_out, layer):
+            copy.wait()
+
+
+def split_bf16(x):
+    high = x.astype(jnp.bfloat16)
+    return high, (x - high.astype(jnp.float32)).astype(jnp.bfloat16)
 
 
 def call(kernel, out, in_specs, scratch=()):
@@ -305,32 +350,34 @@
     perm = log_perm.reshape(layers, rows, columns)
     perm_far = lax.ppermute(perm, "gy", swap)
     rech_far = lax.ppermute(recharge, "gy", swap)
-    perm = pltpu.with_memory_space_constraint(perm, pltpu.HBM)
-    recharge = pltpu.with_memory_space_constraint(recharge, pltpu.HBM)
-    well_cells = pltpu.with_memory_space_constraint(well_cells, pltpu.HBM)
-    well_order_any = pltpu.with_memory_space_constraint(well_order, pltpu.HBM)
-    perm, recharge = call(
-        stage_kernel, (f32(*perm.shape), f32(*recharge.shape)), [HBM, HBM], [pltpu.SemaphoreType.DMA((2, layers))]
-    )(perm, recharge)
-    send = produce(core, well_cells, well_order_any, perm, recharge, perm_far, rech_far)
+    perm, recharge, well_cells, well_order, observed, variances = (
+        pltpu.with_memory_space_constraint(x, pltpu.HBM)
+        for x in (perm, recharge, well_cells, well_order, observed, variances)
+    )
+    perm, recharge, known = call(
+        stage_kernel, (f32(*perm.shape), f32(*recharge.shape), f32(2 * STEPS, parts)), [HBM] * 5,
+        [pltpu.SMEM(well_order.shape, jnp.int32), pltpu.SMEM(observed.shape, jnp.float32)]
+        + [pltpu.SMEM(variances.shape, jnp.float32), pltpu.SemaphoreType.DMA((2, layers))]
+        + [pltpu.SemaphoreType.DMA((3,))],
+    )(perm, recharge, well_order, observed, variances)
+    send = produce(core, well_cells, well_order, perm, recharge, perm_far, rech_far)
     recv = lax.all_to_all(
         send.reshape(parts, -1, 1, columns), "gx", split_axis=0, concat_axis=0, tiled=True
     ).reshape(send.shape)
-    own, give = call(
-        split_kernel, (f32(STEPS, parts), f32(parts * 2 * layers, columns)), [SMEM, VMEM]
-    )(core, recv)
-    other = lax.ppermute(own, "gy", swap)
-    other, give = lax.optimization_barrier((other, give))
+    own = call(wells_kernel, f32(STEPS, parts), [VMEM])(recv)
+    give = call(give_kernel, f32(parts * 2 * layers, columns), [SMEM, VMEM, VMEM])(core, recv, own)
     got = lax.ppermute(give, "gy", swap)
     mix = call(
-        steps_kernel, f32(parts, parts), [SMEM] * 4 + [VMEM] * 2
-    )(core, well_order, observed, variances, own, other)
-    block = pl.BlockSpec((2 * parts, columns), lambda layer: (layer, 0))
-    out = f32(layers * parts * 2, columns)
+        steps_kernel, f32(parts, parts), [VMEM] * 2
+    )(known, own)
+    other_mix = lax.ppermute(mix, "gy", swap)
+    field = (layers, parts * 2, columns)
     post_perm, post_head = pl.pallas_call(
-        apply_kernel, out_shape=(out, out), grid=(layers,),
-        in_specs=[SMEM, VMEM, VMEM, VMEM], out_specs=(block, block), compiler_params=PARAMS,
-    )(core, recv, got, mix)
+        apply_kernel, out_shape=(f32(*field), f32(*field)),
+        in_specs=[SMEM] + [VMEM] * 4, out_specs=(HBM, HBM),
+        scratch_shapes=[pltpu.VMEM(field, jnp.float32)] * 2 + [pltpu.SemaphoreType.DMA((2, layers))],
+        compiler_params=PARAMS,
+    )(core, recv, got, mix, other_mix)
     shape = (layers, parts, 2, columns)
     return post_perm.reshape(shape), post_head.reshape(shape)
 

time: 59.6 us -> 57.9 us (0.971)
  Pallas kernels: 5.91 us -> 4.05 us
    ppermute x1, starting transfers between devices: 9.86 us -> 0.1 us  [body(): other_mix = lax.ppermute(mix, 'gy', swap)]
    ppermute x1, starting transfers between devices: 0.34 us -> 9.91 us  [body(): got = lax.ppermute(give, 'gy', swap)]
    pallas_call x4 -> x5, Pallas kernels: 5.8 us -> 3.94 us  [the longest x1 1.38 us: body(): call(stage_kernel, (f32(*perm.shape), f32(*recharge.shape), f32(2 * STEPS...]
  transfers between devices with their start and end apart: 4 -> 4, of which waited for: 3 -> 3; matrix products, arithmetic and copies ran while one was open for 0% -> 0% of each run, Pallas kernels for 5% -> 4%
where the time goes in v3:
time: 57.9 us; the launch traced here: 57.7 us
  blocking collectives  37.3 us (64%)
  starting transfers between devices  13.4 us (23%)
  Pallas kernels  4.05 us (7%)
  waiting for transfers between devices  2.25 us (4%)
  between operations  0.67 us (1%)
    all_to_all x1, blocking collectives, body(): lax.all_to_all(send.reshape(parts, -1, 1, columns), 'gx', split_axis=0, c...  37.3 us
    ppermute x1, starting transfers between devices, body(): got = lax.ppermute(give, 'gy', swap)  9.91 us
    ppermute x1, starting transfers between devices, body(): perm_far = lax.ppermute(perm, 'gy', swap)  3.33 us
    pallas_call x1, Pallas kernels, body(): call(stage_kernel, (f32(*perm.shape), f32(*recharge.shape), f32(2 * STEPS...  1.38 us
    pallas_call x1, Pallas kernels, body(): pl.pallas_call(apply_kernel, out_shape=(f32(*field), f32(*field)), in_spe...  1.29 us
    ppermute x1, waiting for transfers between devices, body(): other_mix = lax.ppermute(mix, 'gy', swap)  1.24 us
    pallas_call x1, Pallas kernels, body(): mix = call(steps_kernel, f32(parts, parts), [VMEM] * 2)(known, own)  1.18 us
  transfers between devices with their start and end apart: 4, of which 3 were waited for; matrix products, arithmetic and copies ran while one was open for 0% of the time, Pallas kernels for 4%

profile of v3, /device:TPU:1, one launch (start us, length us, event | category | flops | bytes accessed | tf_op | source)
XLA Modules:
  0.0 57.7 jit_solution(7522768318080662161)
XLA Ops:
  0.6 3.3 %collective-permute-start = (f32[4,256,128]{2,1,0:T(8,128)}, f32[4,256,128]{2,1,0:T(8,128)S(1)}, u32[]{:S(2)}, u32[]{:S(2)}) collective-permute-start(f32[4,256,128]{2,1,0:T(8,128)} %bitcast.10), channel_id=1, source_target_pairs={{0,1},{1,0},{2,3},{3,2},{4,5},{5,4},{6,7},{7,6},{8,9},{9,8},{10,11... | collective-permute-start | bytes 1572872 | tf_op jit(solution)/shard_map/ppermute | solution.py:351
  4.0 0.1 collective-permute-start.1
  4.1 1.4 %shard_map.77 = (f32[4,256,128]{2,1,0:T(8,128)S(1)}, f32[4,256,128]{2,1,0:T(8,128)S(1)}, f32[16,128]{1,0:T(8,128)S(1)}) custom-call(f32[4,256,128]{2,1,0:T(8,128)} %bitcast.11, f32[4,256,128]{2,1,0:T(8,128)} %rech_any.1, s32[8]{0:T(128)} %order_any.3, f32[32]{0:T(128)} %obs_any.1, f32[32]{0:T(128)} %var_any.1), custom_call_target="tpu_custom_call" | custom-call | tf_op jit(solution)/shard_map/pallas_call | solution.py:357
  5.4 0.3 collective-permute-done.perm_far
  5.7 0.7 %collective-permute-done.1.rech_far = f32[4,256,128]{2,1,0:T(8,128)S(1)} collective-permute-done((f32[4,256,128]{2,1,0:T(8,128)}, f32[4,256,128]{2,1,0:T(8,128)S(1)}, u32[]{:S(2)}, u32[]{:S(2)}) %collective-permute-start.1) | collective-permute-done | bytes 524320 | tf_op jit(solution)/shard_map/ppermute | solution.py:352
  6.5 0.1 shard_map.78
  6.6 37.3 %all_to_all.5 = f32[128,17,1,128]{3,2,1,0:T(1,128)S(1)} all-to-all(f32[128,17,1,128]{3,2,1,0:T(1,128)S(1)} %bitcast.9), channel_id=1, replica_groups=mesh['gx'=128,'gy'=2] {'gx'}, dimensions={0} | all-to-all | bytes 2228224 | tf_op jit(solution)/shard_map/all_to_all | solution.py:364
  44.0 0.1 shard_map.80
  44.0 9.9 %collective-permute-start.2 = (f32[1024,128]{1,0:T(8,128)S(1)}, f32[1024,128]{1,0:T(8,128)S(1)}, u32[]{:S(2)}, u32[]{:S(2)}) collective-permute-start(f32[1024,128]{1,0:T(8,128)S(1)} %shard_map.80), channel_id=1, source_target_pairs={{0,1},{1,0},{2,3},{3,2},{4,5},{5,4},{6,7},{7,6},{8,9},{9,8},{10,11... | collective-permute-start | bytes 1572872 | tf_op jit(solution)/shard_map/ppermute | solution.py:369
  53.9 1.2 %shard_map.81.own_mix_ref = f32[128,128]{1,0:T(8,128)S(1)} custom-call(f32[16,128]{1,0:T(8,128)S(1)} %get-tuple-element.9.known_ref, f32[8,128]{1,0:T(8,128)S(1)} %shard_map.79.after_ref.own_ref), custom_call_target="tpu_custom_call" | custom-call | tf_op jit(solution)/shard_map/pallas_call | solution.py:370
  55.1 0.1 collective-permute-start.3
  55.2 1.2 %collective-permute-done.3.other_mix_ref = f32[128,128]{1,0:T(8,128)S(1)} collective-permute-done((f32[128,128]{1,0:T(8,128)S(1)}, f32[128,128]{1,0:T(8,128)S(1)}, u32[]{:S(2)}, u32[]{:S(2)}) %collective-permute-start.3) | collective-permute-done | bytes 65568 | tf_op jit(solution)/shard_map/ppermute | solution.py:373
  56.5 0.0 collective-permute-done.2.got_ref
  56.5 1.3 %shard_map.82 = (f32[4,256,128]{2,1,0:T(8,128)}, f32[4,256,128]{2,1,0:T(8,128)}) custom-call(s32[1]{0:T(128)} %bitcast.core_ref, f32[2176,128]{1,0:T(8,128)S(1)} %bitcast.8, f32[1024,128]{1,0:T(8,128)S(1)} %collective-permute-done.2.got_ref, f32[128,128]{1,0:T(8,128)S(1)} %shard_map.81.own_mix_ref, f32[128,128]{1,0:T(8,128)S(1)} %collective-permute-done.3.other_mix_ref), custom_call_target="tpu_custom_call" | custom-call | tf_op jit(solution)/shard_map/pallas_call | solution.py:375
  (1 shorter events, 0.0 us)
Async XLA Ops:
  0.6 5.1 %collective-permute-start = (f32[4,256,128]{2,1,0:T(8,128)}, f32[4,256,128]{2,1,0:T(8,128)S(1)}, u32[]{:S(2)}, u32[]{:S(2)}) collective-permute-start(f32[4,256,128]{2,1,0:T(8,128)} %bitcast.10), channel_id=1, source_target_pairs={{0,1},{1,0},{2,3},{3,2},{4,5},{5,4},{6,7},{7,6},{8,9},{9,8},{10,11... | collective-permute-start | bytes 1572872 | tf_op jit(solution)/shard_map/ppermute | solution.py:351
  4.0 2.5 %collective-permute-start.1 = (f32[4,256,128]{2,1,0:T(8,128)}, f32[4,256,128]{2,1,0:T(8,128)S(1)}, u32[]{:S(2)}, u32[]{:S(2)}) collective-permute-start(f32[4,256,128]{2,1,0:T(8,128)} %rech_any.1), channel_id=1, source_target_pairs={{0,1},{1,0},{2,3},{3,2},{4,5},{5,4},{6,7},{7,6},{8,9},{9,8},{10,11... | collective-permute-start | bytes 1572872 | tf_op jit(solution)/shard_map/ppermute | solution.py:352
  44.0 12.4 %collective-permute-start.2 = (f32[1024,128]{1,0:T(8,128)S(1)}, f32[1024,128]{1,0:T(8,128)S(1)}, u32[]{:S(2)}, u32[]{:S(2)}) collective-permute-start(f32[1024,128]{1,0:T(8,128)S(1)} %shard_map.80), channel_id=1, source_target_pairs={{0,1},{1,0},{2,3},{3,2},{4,5},{5,4},{6,7},{7,6},{8,9},{9,8},{10,11... | collective-permute-start | bytes 1572872 | tf_op jit(solution)/shard_map/ppermute | solution.py:369
  55.1 1.3 %collective-permute-start.3 = (f32[128,128]{1,0:T(8,128)S(1)}, f32[128,128]{1,0:T(8,128)S(1)}, u32[]{:S(2)}, u32[]{:S(2)}) collective-permute-start(f32[128,128]{1,0:T(8,128)S(1)} %shard_map.81.own_mix_ref), channel_id=1, source_target_pairs={{0,1},{1,0},{2,3},{3,2},{4,5},{5,4},{6,7},{7,6},{8,9},{9,8},{10,11... | collective-permute-start | bytes 196616 | tf_op jit(solution)/shard_map/ppermute | solution.py:373

commit v4 on v3

--- a/solution.py
+++ b/solution.py
@@ -234,10 +234,13 @@
 
 def give_kernel(core_ref, recv_ref, after_ref, give_ref):
     members, stride = 128, recv_ref.shape[0] // 128
-    for j in range(8):
-        give_ref[pl.ds(members * j, members), :] = recv_ref[
-            pl.ds(8 * (1 - core_ref[0]) + j, members, stride=stride), :
-        ]
+    for core in range(2):
+        @pl.when(core_ref[0] == core)
+        def _():
+            for j in range(8):
+                give_ref[pl.ds(members * j, members), :] = recv_ref[
+                    pl.ds(8 * (1 - core) + j, members, stride=stride), :
+                ]
 
 
 def steps_kernel(known_ref, own_ref, mix_ref):
@@ -284,34 +287,34 @@
             pltpu.make_async_copy(taken.at[layer], got_out.at[layer], sems.at[1, layer]),
         ]
 
-    for layer in range(layers):
-        x = jnp.concatenate(
-            [recv_ref[pl.ds(8 * core + 2 * layer + r, members, stride=stride), :] for r in range(2)]
-            + [got_ref[pl.ds(members * (2 * layer + r), members), :] for r in range(2)], 1
-        )
-        high, low = split_bf16(x)
-        x = x + jnp.dot(
-            mixes, jnp.concatenate([high, low, high], 0), preferred_element_type=jnp.float32
-        )
-        columns = x.shape[1] // 4
-        for place, ref in enumerate((kept, taken)):
-            for r in range(2):
-                at = (2 * place + r) * columns
-                ref[layer, pl.ds(r, members, stride=2), :] = x[:, at:at + columns]
-
-        @pl.when(core == 0)
-        def _():
-            for copy in copies(head_out, perm_out, layer):
+    def run(first, own_out, got_out):
+        for layer in range(layers):
+            x = jnp.concatenate(
+                [recv_ref[pl.ds(first + 2 * layer + r, members, stride=stride), :] for r in range(2)]
+                + [got_ref[pl.ds(members * (2 * layer + r), members), :] for r in range(2)], 1
+            )
+            high, low = split_bf16(x)
+            x = x + jnp.dot(
+                mixes, jnp.concatenate([high, low, high], 0), preferred_element_type=jnp.float32
+            )
+            columns = x.shape[1] // 4
+            for place, ref in enumerate((kept, taken)):
+                for r in range(2):
+                    at = (2 * place + r) * columns
+                    ref[layer, pl.ds(r, members, stride=2), :] = x[:, at:at + columns]
+            for copy in copies(own_out, got_out, layer):
                 copy.start()
-
-        @pl.when(core == 1)
-        def _():
-            for copy in copies(perm_out, head_out, layer):
-                copy.start()
-
-    for layer in range(layers):
-        for copy in copies(head_out, perm_out, layer):
-            copy.wait()
+        for layer in range(layers):
+            for copy in copies(own_out, got_out, layer):
+                copy.wait()
+
+    @pl.when(core == 0)
+    def _():
+        run(0, head_out, perm_out)
+
+    @pl.when(core == 1)
+    def _():
+        run(8, perm_out, head_out)
 
 
 def split_bf16(x):

time: 57.9 us -> 57.9 us (level)
  no operation moved by 1% of the time
where the time goes in v4:
time: 57.9 us; the launch traced here: 57.8 us
  blocking collectives  37.3 us (64%)
  starting transfers between devices  13.5 us (23%)
  Pallas kernels  4.07 us (7%)
  waiting for transfers between devices  2.25 us (4%)
  between operations  0.67 us (1%)
    all_to_all x1, blocking collectives, body(): lax.all_to_all(send.reshape(parts, -1, 1, columns), 'gx', split_axis=0, c...  37.3 us
    ppermute x1, starting transfers between devices, body(): got = lax.ppermute(give, 'gy', swap)  9.92 us
    ppermute x1, starting transfers between devices, body(): perm_far = lax.ppermute(perm, 'gy', swap)  3.33 us
    pallas_call x1, Pallas kernels, body(): call(stage_kernel, (f32(*perm.shape), f32(*recharge.shape), f32(2 * STEPS...  1.38 us
    pallas_call x1, Pallas kernels, body(): pl.pallas_call(apply_kernel, out_shape=(f32(*field), f32(*field)), in_spe...  1.3 us
    ppermute x1, waiting for transfers between devices, body(): other_mix = lax.ppermute(mix, 'gy', swap)  1.24 us
    pallas_call x1, Pallas kernels, body(): mix = call(steps_kernel, f32(parts, parts), [VMEM] * 2)(known, own)  1.18 us
  transfers between devices with their start and end apart: 4, of which 3 were waited for; matrix products, arithmetic and copies ran while one was open for 0% of the time, Pallas kernels for 4%

profile of v4, /device:TPU:1, one launch (start us, length us, event | category | flops | bytes accessed | tf_op | source)
XLA Modules:
  0.0 57.8 jit_solution(16546986036963651649)
XLA Ops:
  0.6 3.3 %collective-permute-start = (f32[4,256,128]{2,1,0:T(8,128)}, f32[4,256,128]{2,1,0:T(8,128)S(1)}, u32[]{:S(2)}, u32[]{:S(2)}) collective-permute-start(f32[4,256,128]{2,1,0:T(8,128)} %bitcast.10), channel_id=1, source_target_pairs={{0,1},{1,0},{2,3},{3,2},{4,5},{5,4},{6,7},{7,6},{8,9},{9,8},{10,11... | collective-permute-start | bytes 1572872 | tf_op jit(solution)/shard_map/ppermute | solution.py:354
  4.0 0.1 collective-permute-start.1
  4.1 1.4 %shard_map.77 = (f32[4,256,128]{2,1,0:T(8,128)S(1)}, f32[4,256,128]{2,1,0:T(8,128)S(1)}, f32[16,128]{1,0:T(8,128)S(1)}) custom-call(f32[4,256,128]{2,1,0:T(8,128)} %bitcast.11, f32[4,256,128]{2,1,0:T(8,128)} %rech_any.1, s32[8]{0:T(128)} %order_any.3, f32[32]{0:T(128)} %obs_any.1, f32[32]{0:T(128)} %var_any.1), custom_call_target="tpu_custom_call" | custom-call | tf_op jit(solution)/shard_map/pallas_call | solution.py:360
  5.4 0.3 collective-permute-done.perm_far
  5.7 0.7 %collective-permute-done.1.rech_far = f32[4,256,128]{2,1,0:T(8,128)S(1)} collective-permute-done((f32[4,256,128]{2,1,0:T(8,128)}, f32[4,256,128]{2,1,0:T(8,128)S(1)}, u32[]{:S(2)}, u32[]{:S(2)}) %collective-permute-start.1) | collective-permute-done | bytes 524320 | tf_op jit(solution)/shard_map/ppermute | solution.py:355
  6.5 0.1 shard_map.78
  6.6 37.3 %all_to_all.5 = f32[128,17,1,128]{3,2,1,0:T(1,128)S(1)} all-to-all(f32[128,17,1,128]{3,2,1,0:T(1,128)S(1)} %bitcast.9), channel_id=1, replica_groups=mesh['gx'=128,'gy'=2] {'gx'}, dimensions={0} | all-to-all | bytes 2228224 | tf_op jit(solution)/shard_map/all_to_all | solution.py:367
  44.0 0.1 shard_map.80
  44.0 9.9 %collective-permute-start.2 = (f32[1024,128]{1,0:T(8,128)S(1)}, f32[1024,128]{1,0:T(8,128)S(1)}, u32[]{:S(2)}, u32[]{:S(2)}) collective-permute-start(f32[1024,128]{1,0:T(8,128)S(1)} %shard_map.80), channel_id=1, source_target_pairs={{0,1},{1,0},{2,3},{3,2},{4,5},{5,4},{6,7},{7,6},{8,9},{9,8},{10,11... | collective-permute-start | bytes 1572872 | tf_op jit(solution)/shard_map/ppermute | solution.py:372
  53.9 1.2 %shard_map.81.own_mix_ref = f32[128,128]{1,0:T(8,128)S(1)} custom-call(f32[16,128]{1,0:T(8,128)S(1)} %get-tuple-element.9.known_ref, f32[8,128]{1,0:T(8,128)S(1)} %shard_map.79.after_ref.own_ref), custom_call_target="tpu_custom_call" | custom-call | tf_op jit(solution)/shard_map/pallas_call | solution.py:373
  55.1 0.1 collective-permute-start.3
  55.2 1.2 %collective-permute-done.3.other_mix_ref = f32[128,128]{1,0:T(8,128)S(1)} collective-permute-done((f32[128,128]{1,0:T(8,128)S(1)}, f32[128,128]{1,0:T(8,128)S(1)}, u32[]{:S(2)}, u32[]{:S(2)}) %collective-permute-start.3) | collective-permute-done | bytes 65568 | tf_op jit(solution)/shard_map/ppermute | solution.py:376
  56.5 0.0 collective-permute-done.2.got_ref
  56.5 1.3 %shard_map.82 = (f32[4,256,128]{2,1,0:T(8,128)}, f32[4,256,128]{2,1,0:T(8,128)}) custom-call(s32[1]{0:T(128)} %bitcast.core_ref, f32[2176,128]{1,0:T(8,128)S(1)} %bitcast.8, f32[1024,128]{1,0:T(8,128)S(1)} %collective-permute-done.2.got_ref, f32[128,128]{1,0:T(8,128)S(1)} %shard_map.81.own_mix_ref, f32[128,128]{1,0:T(8,128)S(1)} %collective-permute-done.3.other_mix_ref), custom_call_target="tpu_custom_call" | custom-call | tf_op jit(solution)/shard_map/pallas_call | solution.py:378
  (1 shorter events, 0.0 us)
Async XLA Ops:
  0.6 5.1 %collective-permute-start = (f32[4,256,128]{2,1,0:T(8,128)}, f32[4,256,128]{2,1,0:T(8,128)S(1)}, u32[]{:S(2)}, u32[]{:S(2)}) collective-permute-start(f32[4,256,128]{2,1,0:T(8,128)} %bitcast.10), channel_id=1, source_target_pairs={{0,1},{1,0},{2,3},{3,2},{4,5},{5,4},{6,7},{7,6},{8,9},{9,8},{10,11... | collective-permute-start | bytes 1572872 | tf_op jit(solution)/shard_map/ppermute | solution.py:354
  4.0 2.5 %collective-permute-start.1 = (f32[4,256,128]{2,1,0:T(8,128)}, f32[4,256,128]{2,1,0:T(8,128)S(1)}, u32[]{:S(2)}, u32[]{:S(2)}) collective-permute-start(f32[4,256,128]{2,1,0:T(8,128)} %rech_any.1), channel_id=1, source_target_pairs={{0,1},{1,0},{2,3},{3,2},{4,5},{5,4},{6,7},{7,6},{8,9},{9,8},{10,11... | collective-permute-start | bytes 1572872 | tf_op jit(solution)/shard_map/ppermute | solution.py:355
  44.0 12.5 %collective-permute-start.2 = (f32[1024,128]{1,0:T(8,128)S(1)}, f32[1024,128]{1,0:T(8,128)S(1)}, u32[]{:S(2)}, u32[]{:S(2)}) collective-permute-start(f32[1024,128]{1,0:T(8,128)S(1)} %shard_map.80), channel_id=1, source_target_pairs={{0,1},{1,0},{2,3},{3,2},{4,5},{5,4},{6,7},{7,6},{8,9},{9,8},{10,11... | collective-permute-start | bytes 1572872 | tf_op jit(solution)/shard_map/ppermute | solution.py:372
  55.1 1.3 %collective-permute-start.3 = (f32[128,128]{1,0:T(8,128)S(1)}, f32[128,128]{1,0:T(8,128)S(1)}, u32[]{:S(2)}, u32[]{:S(2)}) collective-permute-start(f32[128,128]{1,0:T(8,128)S(1)} %shard_map.81.own_mix_ref), channel_id=1, source_target_pairs={{0,1},{1,0},{2,3},{3,2},{4,5},{5,4},{6,7},{7,6},{8,9},{9,8},{10,11... | collective-permute-start | bytes 196616 | tf_op jit(solution)/shard_map/ppermute | solution.py:376

commit v5 on v4

--- a/solution.py
+++ b/solution.py
@@ -195,36 +195,29 @@
         send_ref[pl.ds(stride * g + stride - 1, 8, stride=stride), :] = block
 
 
-def produce_kernel(
-    core_ref, cells_any, order_any, perm_ref, rech_ref, perm_far, rech_far, send_ref,
+def heads_kernel(
+    cells_any, order_any, perm_ref, rech_ref, perm_far, rech_far, send_ref,
     cells_ref, order_ref, sems, *scratch,
 ):
-    layers, rows, columns = perm_ref.shape
-
-    @pl.when(core_ref[0] == 0)
-    def _():
-        copies = [
-            pltpu.make_async_copy(cells_any, cells_ref, sems.at[0]),
-            pltpu.make_async_copy(order_any, order_ref, sems.at[1]),
-        ]
-        for copy in copies:
-            copy.start()
-        last = jacobi((perm_ref, perm_far), (rech_ref, rech_far), send_ref, *scratch)
-        for copy in copies:
-            copy.wait()
-        put_wells(last, cells_ref, order_ref, send_ref)
-
-    @pl.when(core_ref[0] == 1)
-    def _():
-        stride = send_ref.shape[0] * 2 // rows
-        both = (perm_far, perm_ref)
-        pack_rows(
-            lambda half, layer, start: both[half][layer, pl.ds(start, 8, stride=2), :],
-            send_ref, layers, rows, stride,
-        )
-        blank = jnp.zeros((8, columns), jnp.float32)
-        for g in range(0, rows // 2, 8):
-            send_ref[pl.ds(stride * g + stride - 1, 8, stride=stride), :] = blank
+    copies = [
+        pltpu.make_async_copy(cells_any, cells_ref, sems.at[0]),
+        pltpu.make_async_copy(order_any, order_ref, sems.at[1]),
+    ]
+    for copy in copies:
+        copy.start()
+    last = jacobi((perm_ref, perm_far), (rech_ref, rech_far), send_ref, *scratch)
+    for copy in copies:
+        copy.wait()
+    put_wells(last, cells_ref, order_ref, send_ref)
+
+
+def pack_kernel(perm_ref, perm_far, send_ref):
+    layers, rows, _ = perm_ref.shape
+    both = (perm_far, perm_ref)
+    pack_rows(
+        lambda half, layer, start: both[half][layer, pl.ds(start, 8, stride=2), :],
+        send_ref, layers, rows, 4 * layers,
+    )
 
 
 def wells_kernel(recv_ref, wells_ref):
@@ -239,7 +232,7 @@
         def _():
             for j in range(8):
                 give_ref[pl.ds(members * j, members), :] = recv_ref[
-                    pl.ds(8 * (1 - core) + j, members, stride=stride), :
+                    pl.ds(8 * (1 - core) + j, members, stride=stride - core), :
                 ]
 
 
@@ -287,10 +280,10 @@
             pltpu.make_async_copy(taken.at[layer], got_out.at[layer], sems.at[1, layer]),
         ]
 
-    def run(first, own_out, got_out):
+    def run(first, step, own_out, got_out):
         for layer in range(layers):
             x = jnp.concatenate(
-                [recv_ref[pl.ds(first + 2 * layer + r, members, stride=stride), :] for r in range(2)]
+                [recv_ref[pl.ds(first + 2 * layer + r, members, stride=step), :] for r in range(2)]
                 + [got_ref[pl.ds(members * (2 * layer + r), members), :] for r in range(2)], 1
             )
             high, low = split_bf16(x)
@@ -310,11 +303,11 @@
 
     @pl.when(core == 0)
     def _():
-        run(0, head_out, perm_out)
+        run(0, stride, head_out, perm_out)
 
     @pl.when(core == 1)
     def _():
-        run(8, perm_out, head_out)
+        run(8, stride - 1, perm_out, head_out)
 
 
 def split_bf16(x):
@@ -334,15 +327,38 @@
     return jax.ShapeDtypeStruct(shape, jnp.float32)
 
 
-def produce(core, cells, order, perm, rech, perm_far, rech_far):
+def exchange(send, parts):
+    return lax.all_to_all(
+        send.reshape(parts, -1, 1, send.shape[1]), "gx", split_axis=0, concat_axis=0, tiled=True
+    ).reshape(send.shape)
+
+
+def heads_part(cells, order, perm, rech, perm_far, rech_far, perm_recv):
     layers, rows, columns = perm.shape
     field = pltpu.VMEM((2, layers, rows, columns), jnp.float32)
     padded = pltpu.VMEM((2, layers, rows + 2 * PAD, columns), jnp.float32)
-    return call(
-        produce_kernel, f32(rows // 2 * (4 * layers + 1), columns), [SMEM, HBM, HBM] + [VMEM] * 4,
+    send = call(
+        heads_kernel, f32(rows // 2 * (4 * layers + 1), columns), [HBM, HBM] + [VMEM] * 4,
         [pltpu.SMEM(cells.shape, jnp.int32), pltpu.SMEM(order.shape, jnp.int32), pltpu.SemaphoreType.DMA((2,))]
         + [padded, padded] + [field] * 8 + [padded, padded],
-    )(core, cells, order, perm, rech, perm_far, rech_far)
+    )(cells, order, perm, rech, perm_far, rech_far)
+    return exchange(send, rows // 2)
+
+
+def rest_part(cells, order, perm, rech, perm_far, rech_far, perm_recv):
+    rows, columns = perm.shape[1:]
+    return jnp.concatenate([perm_recv, jnp.zeros((rows // 2, columns), jnp.float32)], 0)
+
+
+def perm_part(perm, perm_far):
+    layers, rows, columns = perm.shape
+    send = call(pack_kernel, f32(rows // 2 * 4 * layers, columns), [VMEM, VMEM])(perm, perm_far)
+    return exchange(send, rows // 2)
+
+
+def no_part(perm, perm_far):
+    layers, rows, columns = perm.shape
+    return jnp.zeros((rows // 2 * 4 * layers, columns), jnp.float32)
 
 
 def body(log_perm, recharge, well_cells, observed, variances, well_order):
@@ -363,10 +379,11 @@
         + [pltpu.SMEM(variances.shape, jnp.float32), pltpu.SemaphoreType.DMA((2, layers))]
         + [pltpu.SemaphoreType.DMA((3,))],
     )(perm, recharge, well_order, observed, variances)
-    send = produce(core, well_cells, well_order, perm, recharge, perm_far, rech_far)
-    recv = lax.all_to_all(
-        send.reshape(parts, -1, 1, columns), "gx", split_axis=0, concat_axis=0, tiled=True
-    ).reshape(send.shape)
+    perm_recv = lax.cond(core[0] == 1, perm_part, no_part, perm, perm_far)
+    recv = lax.cond(
+        core[0] == 0, heads_part, rest_part,
+        well_cells, well_order, perm, recharge, perm_far, rech_far, perm_recv,
+    )
     own = call(wells_kernel, f32(STEPS, parts), [VMEM])(recv)
     give = call(give_kernel, f32(parts * 2 * layers, columns), [SMEM, VMEM, VMEM])(core, recv, own)
     got = lax.ppermute(give, "gy", swap)

time: 57.9 us -> 56.9 us (0.983)
  blocking collectives: 37.3 us -> 35.2 us
  starting transfers between devices: 13.5 us -> 14.7 us
  waiting for transfers between devices: 2.25 us -> 1.51 us
  Pallas kernels: 4.07 us -> 4.68 us
    all_to_all x1, blocking collectives: 37.3 us -> 35.2 us  [exchange(): lax.all_to_all(send.reshape(parts, -1, 1, send.shape[1]), 'gx', split_axi...]
    ppermute x1, starting transfers between devices: 9.92 us -> 11.2 us  [body(): got = lax.ppermute(give, 'gy', swap)]
    ppermute x1, waiting for transfers between devices: 0.75 us -> 0.01 us  [body(): rech_far = lax.ppermute(recharge, 'gy', swap)]
  transfers between devices with their start and end apart: 4 -> 4, of which waited for: 3 -> 2; matrix products, arithmetic and copies ran while one was open for 0% -> 0% of each run, Pallas kernels for 4% -> 5%
where the time goes in v5:
time: 56.9 us; the launch traced here: 56.8 us
  blocking collectives  35.2 us (62%)
  starting transfers between devices  14.7 us (26%)
  Pallas kernels  4.68 us (8%)
  waiting for transfers between devices  1.51 us (3%)
  between operations  0.67 us (1%)
    all_to_all x1, blocking collectives, exchange(): lax.all_to_all(send.reshape(parts, -1, 1, send.shape[1]), 'gx', split_axi...  35.2 us
    ppermute x1, starting transfers between devices, body(): got = lax.ppermute(give, 'gy', swap)  11.2 us
    ppermute x1, starting transfers between devices, body(): perm_far = lax.ppermute(perm, 'gy', swap)  3.33 us
    pallas_call x1, Pallas kernels, body(): call(stage_kernel, (f32(*perm.shape), f32(*recharge.shape), f32(2 * STEPS...  1.38 us
    pallas_call x1, Pallas kernels, body(): pl.pallas_call(apply_kernel, out_shape=(f32(*field), f32(*field)), in_spe...  1.36 us
    ppermute x1, waiting for transfers between devices, body(): other_mix = lax.ppermute(mix, 'gy', swap)  1.24 us
    pallas_call x1, Pallas kernels, body(): mix = call(steps_kernel, f32(parts, parts), [VMEM] * 2)(known, own)  1.17 us
  transfers between devices with their start and end apart: 4, of which 2 were waited for; matrix products, arithmetic and copies ran while one was open for 0% of the time, Pallas kernels for 5%

profile of v5, /device:TPU:1, one launch (start us, length us, event | category | flops | bytes accessed | tf_op | source)
XLA Modules:
  0.0 56.8 jit_solution(3669602922525415218)
XLA Ops:
  0.6 3.3 %collective-permute-start = (f32[4,256,128]{2,1,0:T(8,128)}, f32[4,256,128]{2,1,0:T(8,128)S(1)}, u32[]{:S(2)}, u32[]{:S(2)}) collective-permute-start(f32[4,256,128]{2,1,0:T(8,128)} %bitcast.14), channel_id=1, source_target_pairs={{0,1},{1,0},{2,3},{3,2},{4,5},{5,4},{6,7},{7,6},{8,9},{9,8},{10,11... | collective-permute-start | bytes 1572872 | tf_op jit(solution)/shard_map/ppermute | solution.py:370
  4.0 0.1 collective-permute-start.1
  4.1 1.4 %shard_map.78 = (f32[4,256,128]{2,1,0:T(8,128)S(1)}, f32[4,256,128]{2,1,0:T(8,128)S(1)}, f32[16,128]{1,0:T(8,128)S(1)}) custom-call(f32[4,256,128]{2,1,0:T(8,128)} %bitcast.15, f32[4,256,128]{2,1,0:T(8,128)} %rech_any.1, s32[8]{0:T(128)} %order_any.1, f32[32]{0:T(128)} %obs_any.1, f32[32]{0:T(128)} %var_any.1), custom_call_target="tpu_custom_call" | custom-call | tf_op jit(solution)/shard_map/pallas_call | solution.py:376
  5.4 0.3 collective-permute-done
  5.7 35.7 %conditional.2 = (f32[2048,128]{1,0:T(8,128)S(1)}) conditional(s32[]{:T(128)} %convert_element_type.7, () %tuple.20, (f32[4,256,128]{2,1,0:T(8,128)S(1)}, f32[4,256,128]{2,1,0:T(8,128)S(1)}) %tuple.21), branch_computations={%region_0.0_spmd, %region_1.0_spmd} | conditional | bytes 2097160 | solution.py:382
  5.7 0.5 branch_1_fun.2
  6.2 35.2 %all_to_all.8 = f32[128,16,1,128]{3,1,2,0:T(8,128)S(1)} all-to-all(f32[128,16,1,128]{3,1,2,0:T(8,128)S(1)} %bitcast.11), channel_id=1, replica_groups=mesh['gx'=128,'gy'=2] {'gx'}, dimensions={0} | all-to-all | bytes 2097152 | tf_op jit(solution)/shard_map/cond/branch_1_fun/all_to_all | solution.py:331
  41.4 0.0 collective-permute-done.1
  41.4 0.1 conditional.3
  41.4 0.1 concatenate.2
  41.5 0.2 shard_map.80
  41.7 11.2 %collective-permute-start.2 = (f32[1024,128]{1,0:T(8,128)S(1)}, f32[1024,128]{1,0:T(8,128)S(1)}, u32[]{:S(2)}, u32[]{:S(2)}) collective-permute-start(f32[1024,128]{1,0:T(8,128)S(1)} %shard_map.80), channel_id=1, source_target_pairs={{0,1},{1,0},{2,3},{3,2},{4,5},{5,4},{6,7},{7,6},{8,9},{9,8},{10,11... | collective-permute-start | bytes 1572872 | tf_op jit(solution)/shard_map/ppermute | solution.py:389
  52.9 1.2 %shard_map.81.own_mix_ref = f32[128,128]{1,0:T(8,128)S(1)} custom-call(f32[16,128]{1,0:T(8,128)S(1)} %get-tuple-element.40.known_ref, f32[8,128]{1,0:T(8,128)S(1)} %shard_map.79.after_ref.own_ref), custom_call_target="tpu_custom_call" | custom-call | tf_op jit(solution)/shard_map/pallas_call | solution.py:390
  54.1 0.1 collective-permute-start.3
  54.2 1.2 %collective-permute-done.3.other_mix_ref = f32[128,128]{1,0:T(8,128)S(1)} collective-permute-done((f32[128,128]{1,0:T(8,128)S(1)}, f32[128,128]{1,0:T(8,128)S(1)}, u32[]{:S(2)}, u32[]{:S(2)}) %collective-permute-start.3) | collective-permute-done | bytes 65568 | tf_op jit(solution)/shard_map/ppermute | solution.py:393
  55.4 0.0 collective-permute-done.2.got_ref
  55.4 1.4 %shard_map.82 = (f32[4,256,128]{2,1,0:T(8,128)}, f32[4,256,128]{2,1,0:T(8,128)}) custom-call(s32[1]{0:T(128)} %bitcast.6.core_ref, f32[2176,128]{1,0:T(8,128)S(1)} %get-tuple-element.46.recv_ref, f32[1024,128]{1,0:T(8,128)S(1)} %collective-permute-done.2.got_ref, f32[128,128]{1,0:T(8,128)S(1)} %shard_map.81.own_mix_ref, ...), custom_call_target="tpu_custom_call" | custom-call | tf_op jit(solution)/shard_map/pallas_call | solution.py:395
  (1 shorter events, 0.0 us)
Async XLA Ops:
  0.6 5.1 %collective-permute-start = (f32[4,256,128]{2,1,0:T(8,128)}, f32[4,256,128]{2,1,0:T(8,128)S(1)}, u32[]{:S(2)}, u32[]{:S(2)}) collective-permute-start(f32[4,256,128]{2,1,0:T(8,128)} %bitcast.14), channel_id=1, source_target_pairs={{0,1},{1,0},{2,3},{3,2},{4,5},{5,4},{6,7},{7,6},{8,9},{9,8},{10,11... | collective-permute-start | bytes 1572872 | tf_op jit(solution)/shard_map/ppermute | solution.py:370
  4.0 37.4 %collective-permute-start.1 = (f32[4,256,128]{2,1,0:T(8,128)}, f32[4,256,128]{2,1,0:T(8,128)S(1)}, u32[]{:S(2)}, u32[]{:S(2)}) collective-permute-start(f32[4,256,128]{2,1,0:T(8,128)} %rech_any.1), channel_id=1, source_target_pairs={{0,1},{1,0},{2,3},{3,2},{4,5},{5,4},{6,7},{7,6},{8,9},{9,8},{10,11... | collective-permute-start | bytes 1572872 | tf_op jit(solution)/shard_map/ppermute | solution.py:371
  41.7 13.7 %collective-permute-start.2 = (f32[1024,128]{1,0:T(8,128)S(1)}, f32[1024,128]{1,0:T(8,128)S(1)}, u32[]{:S(2)}, u32[]{:S(2)}) collective-permute-start(f32[1024,128]{1,0:T(8,128)S(1)} %shard_map.80), channel_id=1, source_target_pairs={{0,1},{1,0},{2,3},{3,2},{4,5},{5,4},{6,7},{7,6},{8,9},{9,8},{10,11... | collective-permute-start | bytes 1572872 | tf_op jit(solution)/shard_map/ppermute | solution.py:389
  54.1 1.3 %collective-permute-start.3 = (f32[128,128]{1,0:T(8,128)S(1)}, f32[128,128]{1,0:T(8,128)S(1)}, u32[]{:S(2)}, u32[]{:S(2)}) collective-permute-start(f32[128,128]{1,0:T(8,128)S(1)} %shard_map.81.own_mix_ref), channel_id=1, source_target_pairs={{0,1},{1,0},{2,3},{3,2},{4,5},{5,4},{6,7},{7,6},{8,9},{9,8},{10,11... | collective-permute-start | bytes 196616 | tf_op jit(solution)/shard_map/ppermute | solution.py:393

commit v6 on v5

--- a/solution.py
+++ b/solution.py
@@ -12,6 +12,7 @@
 VERT = 0.1
 LEAK = 0.1
 PAD = 8
+PLANE = 16
 CHUNK = 32
 HIGHEST = lax.Precision.HIGHEST
 
@@ -353,7 +354,19 @@
 def perm_part(perm, perm_far):
     layers, rows, columns = perm.shape
     send = call(pack_kernel, f32(rows // 2 * 4 * layers, columns), [VMEM, VMEM])(perm, perm_far)
-    return exchange(send, rows // 2)
+    parts, depth = rows // 2, rows // 2 // PLANE
+    along_z = [[z * PLANE + spot for z in range(depth)] for spot in range(PLANE)]
+    in_plane = [[z * PLANE + spot for spot in range(PLANE)] for z in range(depth)]
+
+    def stage(x, groups):
+        return lax.all_to_all(
+            x.reshape(parts, -1, 1, columns), "gx", split_axis=0, concat_axis=0, tiled=True,
+            axis_index_groups=groups,
+        )
+
+    x = stage(send, along_z).reshape(depth, PLANE, -1, columns).swapaxes(0, 1)
+    x = stage(x, in_plane).reshape(PLANE, depth, -1, columns).swapaxes(0, 1)
+    return x.reshape(send.shape)
 
 
 def no_part(perm, perm_far):

time: 56.9 us -> 55.7 us (0.979)
  starting transfers between devices: 14.7 us -> 4.1 us
  blocking collectives: 35.2 us -> 44.6 us
    ppermute x1, starting transfers between devices: 11.2 us -> 0.09 us  [body(): got = lax.ppermute(give, 'gy', swap)]
    all_to_all x1 -> x2, blocking collectives: 35.2 us -> 44.6 us  [stage(): lax.all_to_all(x.reshape(parts, -1, 1, columns), 'gx', split_axis=0, conc...]
  transfers between devices with their start and end apart: 4 -> 4, of which waited for: 2 -> 2; matrix products, arithmetic and copies ran while one was open for 0% -> 0% of each run, Pallas kernels for 5% -> 6%
where the time goes in v6:
time: 55.7 us; the launch traced here: 55.5 us
  blocking collectives  44.6 us (80%)
  Pallas kernels  4.67 us (8%)
  starting transfers between devices  4.1 us (7%)
  waiting for transfers between devices  1.17 us (2%)
  between operations  0.69 us (1%)
    all_to_all x2, blocking collectives, stage(): lax.all_to_all(x.reshape(parts, -1, 1, columns), 'gx', split_axis=0, conc...  44.6 us
    ppermute x1, starting transfers between devices, body(): perm_far = lax.ppermute(perm, 'gy', swap)  3.33 us
    pallas_call x1, Pallas kernels, body(): call(stage_kernel, (f32(*perm.shape), f32(*recharge.shape), f32(2 * STEPS...  1.38 us
    pallas_call x1, Pallas kernels, body(): pl.pallas_call(apply_kernel, out_shape=(f32(*field), f32(*field)), in_spe...  1.34 us
    pallas_call x1, Pallas kernels, body(): mix = call(steps_kernel, f32(parts, parts), [VMEM] * 2)(known, own)  1.18 us
  transfers between devices with their start and end apart: 4, of which 2 were waited for; matrix products, arithmetic and copies ran while one was open for 0% of the time, Pallas kernels for 6%

profile of v6, /device:TPU:1, one launch (start us, length us, event | category | flops | bytes accessed | tf_op | source)
XLA Modules:
  0.0 55.5 jit_solution(13827821040928681610)
XLA Ops:
  0.6 3.3 %collective-permute-start = (f32[4,256,128]{2,1,0:T(8,128)}, f32[4,256,128]{2,1,0:T(8,128)S(1)}, u32[]{:S(2)}, u32[]{:S(2)}) collective-permute-start(f32[4,256,128]{2,1,0:T(8,128)} %bitcast.26), channel_id=1, source_target_pairs={{0,1},{1,0},{2,3},{3,2},{4,5},{5,4},{6,7},{7,6},{8,9},{9,8},{10,11... | collective-permute-start | bytes 1572872 | tf_op jit(solution)/shard_map/ppermute | solution.py:383
  4.0 0.1 collective-permute-start.1
  4.1 1.4 %shard_map.78 = (f32[4,256,128]{2,1,0:T(8,128)S(1)}, f32[4,256,128]{2,1,0:T(8,128)S(1)}, f32[16,128]{1,0:T(8,128)S(1)}) custom-call(f32[4,256,128]{2,1,0:T(8,128)} %bitcast.27, f32[4,256,128]{2,1,0:T(8,128)} %rech_any.1, s32[8]{0:T(128)} %order_any.1, f32[32]{0:T(128)} %obs_any.1, f32[32]{0:T(128)} %var_any.1), custom_call_target="tpu_custom_call" | custom-call | tf_op jit(solution)/shard_map/pallas_call | solution.py:389
  5.4 0.3 collective-permute-done
  5.7 45.3 %conditional.2 = (f32[2048,128]{1,0:T(8,128)S(1)}) conditional(s32[]{:T(128)} %convert_element_type.7, () %tuple.20, (f32[4,256,128]{2,1,0:T(8,128)S(1)}, f32[4,256,128]{2,1,0:T(8,128)S(1)}) %tuple.21), branch_computations={%region_0.0_spmd, %region_1.0_spmd} | conditional | bytes 8388616 | solution.py:395
  5.7 0.5 branch_1_fun.2
  6.2 24.0 %all_to_all.12 = f32[128,16,1,128]{3,1,2,0:T(8,128)S(1)} all-to-all(f32[128,16,1,128]{3,1,2,0:T(8,128)S(1)} %bitcast.20), channel_id=1, replica_groups={{0,32,64,96,128,160,192,224},{2,34,66,98,130,162,194,226},{4,36,68,100,..., dimensions={0} | all-to-all | bytes 2097152 | tf_op jit(solution)/shard_map/cond/branch_1_fun/all_to_all | solution.py:362
  30.3 0.1 copy.12
  30.4 20.6 %all_to_all.13 = f32[128,16,1,128]{3,1,2,0:T(8,128)S(1)} all-to-all(f32[128,16,1,128]{3,1,2,0:T(8,128)S(1)} %bitcast.24), channel_id=1, replica_groups={{0,2,4,6,8,10,12,14,16,18,20,22,24,26,28,30},{32,34,36,38,40,42,44,46,4..., dimensions={0} | all-to-all | bytes 2097152 | tf_op jit(solution)/shard_map/cond/branch_1_fun/all_to_all | solution.py:362
  51.0 0.1 copy.14
  51.1 0.0 collective-permute-done.1
  51.1 0.1 conditional.3
  51.1 0.1 concatenate.2
  51.2 0.2 shard_map.80
  51.4 0.1 collective-permute-start.2
  51.5 1.2 %shard_map.81.own_mix_ref = f32[128,128]{1,0:T(8,128)S(1)} custom-call(f32[16,128]{1,0:T(8,128)S(1)} %get-tuple-element.40.known_ref, f32[8,128]{1,0:T(8,128)S(1)} %shard_map.79.after_ref.own_ref), custom_call_target="tpu_custom_call" | custom-call | tf_op jit(solution)/shard_map/pallas_call | solution.py:403
  52.7 0.6 %collective-permute-start.3 = (f32[128,128]{1,0:T(8,128)S(1)}, f32[128,128]{1,0:T(8,128)S(1)}, u32[]{:S(2)}, u32[]{:S(2)}) collective-permute-start(f32[128,128]{1,0:T(8,128)S(1)} %shard_map.81.own_mix_ref), channel_id=1, source_target_pairs={{0,1},{1,0},{2,3},{3,2},{4,5},{5,4},{6,7},{7,6},{8,9},{9,8},{10,11... | collective-permute-start | bytes 196616 | tf_op jit(solution)/shard_map/ppermute | solution.py:406
  53.3 0.9 %collective-permute-done.3.other_mix_ref = f32[128,128]{1,0:T(8,128)S(1)} collective-permute-done((f32[128,128]{1,0:T(8,128)S(1)}, f32[128,128]{1,0:T(8,128)S(1)}, u32[]{:S(2)}, u32[]{:S(2)}) %collective-permute-start.3) | collective-permute-done | bytes 65568 | tf_op jit(solution)/shard_map/ppermute | solution.py:406
  54.2 0.0 collective-permute-done.2.got_ref
  54.2 1.3 %shard_map.82 = (f32[4,256,128]{2,1,0:T(8,128)}, f32[4,256,128]{2,1,0:T(8,128)}) custom-call(s32[1]{0:T(128)} %bitcast.15.core_ref, f32[2176,128]{1,0:T(8,128)S(1)} %get-tuple-element.46.recv_ref, f32[1024,128]{1,0:T(8,128)S(1)} %collective-permute-done.2.got_ref, f32[128,128]{1,0:T(8,128)S(1)} %shard_map.81.own_mix_ref, ...), custom_call_target="tpu_custom_call" | custom-call | tf_op jit(solution)/shard_map/pallas_call | solution.py:408
  (1 shorter events, 0.0 us)
Async XLA Ops:
  0.6 5.1 %collective-permute-start = (f32[4,256,128]{2,1,0:T(8,128)}, f32[4,256,128]{2,1,0:T(8,128)S(1)}, u32[]{:S(2)}, u32[]{:S(2)}) collective-permute-start(f32[4,256,128]{2,1,0:T(8,128)} %bitcast.26), channel_id=1, source_target_pairs={{0,1},{1,0},{2,3},{3,2},{4,5},{5,4},{6,7},{7,6},{8,9},{9,8},{10,11... | collective-permute-start | bytes 1572872 | tf_op jit(solution)/shard_map/ppermute | solution.py:383
  4.0 47.1 %collective-permute-start.1 = (f32[4,256,128]{2,1,0:T(8,128)}, f32[4,256,128]{2,1,0:T(8,128)}, u32[]{:S(2)}, u32[]{:S(2)}) collective-permute-start(f32[4,256,128]{2,1,0:T(8,128)} %rech_any.1), channel_id=1, source_target_pairs={{0,1},{1,0},{2,3},{3,2},{4,5},{5,4},{6,7},{7,6},{8,9},{9,8},{10,11... | collective-permute-start | bytes 1572872 | tf_op jit(solution)/shard_map/ppermute | solution.py:384
  51.4 2.8 %collective-permute-start.2 = (f32[1024,128]{1,0:T(8,128)S(1)}, f32[1024,128]{1,0:T(8,128)S(1)}, u32[]{:S(2)}, u32[]{:S(2)}) collective-permute-start(f32[1024,128]{1,0:T(8,128)S(1)} %shard_map.80), channel_id=1, source_target_pairs={{0,1},{1,0},{2,3},{3,2},{4,5},{5,4},{6,7},{7,6},{8,9},{9,8},{10,11... | collective-permute-start | bytes 1572872 | tf_op jit(solution)/shard_map/ppermute | solution.py:402
  52.7 1.5 %collective-permute-start.3 = (f32[128,128]{1,0:T(8,128)S(1)}, f32[128,128]{1,0:T(8,128)S(1)}, u32[]{:S(2)}, u32[]{:S(2)}) collective-permute-start(f32[128,128]{1,0:T(8,128)S(1)} %shard_map.81.own_mix_ref), channel_id=1, source_target_pairs={{0,1},{1,0},{2,3},{3,2},{4,5},{5,4},{6,7},{7,6},{8,9},{9,8},{10,11... | collective-permute-start | bytes 196616 | tf_op jit(solution)/shard_map/ppermute | solution.py:406

commit v7 on v6

--- a/solution.py
+++ b/solution.py
@@ -19,6 +19,7 @@
 VMEM = pl.BlockSpec(memory_space=pltpu.VMEM)
 SMEM = pl.BlockSpec(memory_space=pltpu.SMEM)
 HBM = pl.BlockSpec(memory_space=pltpu.HBM)
+ANY = pl.BlockSpec(memory_space=pl.ANY)
 PARAMS = pltpu.CompilerParams(vmem_limit_bytes=48 * 1024 * 1024)
 
 
@@ -61,7 +62,7 @@
                     send_ref[pl.ds(stride * g + row, 8, stride=stride), :] = load(half, layer, 2 * g + r)
 
 
-def jacobi(perm, rech, send_ref, inv, rowt, vert, cn, cs, cw, ce, cu, cd, base, head_a, head_b):
+def jacobi(perm, rech, rech_copy, send_ref, inv, rowt, vert, cn, cs, cw, ce, cu, cd, base, head_a, head_b):
     layers, rows, columns = perm[0].shape
     lane = lax.broadcasted_iota(jnp.int32, (CHUNK, columns), 1)
     west_end, east_end = lane == 0, lane == columns - 1
@@ -138,6 +139,7 @@
                 base[half, layer, part, :] = first
                 head_a[half, layer, pl.ds(PAD + r, CHUNK), :] = first
 
+    rech_copy.wait()
     chunks(weigh)
 
     def relax(old, new):
@@ -197,16 +199,18 @@
 
 
 def heads_kernel(
-    cells_any, order_any, perm_ref, rech_ref, perm_far, rech_far, send_ref,
-    cells_ref, order_ref, sems, *scratch,
+    cells_any, order_any, perm_ref, rech_ref, perm_far, rech_any, send_ref,
+    cells_ref, order_ref, rech_far, sems, *scratch,
 ):
     copies = [
         pltpu.make_async_copy(cells_any, cells_ref, sems.at[0]),
         pltpu.make_async_copy(order_any, order_ref, sems.at[1]),
     ]
+    rech_copy = pltpu.make_async_copy(rech_any, rech_far, sems.at[2])
+    rech_copy.start()
     for copy in copies:
         copy.start()
-    last = jacobi((perm_ref, perm_far), (rech_ref, rech_far), send_ref, *scratch)
+    last = jacobi((perm_ref, perm_far), (rech_ref, rech_far), rech_copy, send_ref, *scratch)
     for copy in copies:
         copy.wait()
     put_wells(last, cells_ref, order_ref, send_ref)
@@ -339,8 +343,9 @@
     field = pltpu.VMEM((2, layers, rows, columns), jnp.float32)
     padded = pltpu.VMEM((2, layers, rows + 2 * PAD, columns), jnp.float32)
     send = call(
-        heads_kernel, f32(rows // 2 * (4 * layers + 1), columns), [HBM, HBM] + [VMEM] * 4,
-        [pltpu.SMEM(cells.shape, jnp.int32), pltpu.SMEM(order.shape, jnp.int32), pltpu.SemaphoreType.DMA((2,))]
+        heads_kernel, f32(rows // 2 * (4 * layers + 1), columns), [HBM, HBM] + [VMEM] * 3 + [ANY],
+        [pltpu.SMEM(cells.shape, jnp.int32), pltpu.SMEM(order.shape, jnp.int32)]
+        + [pltpu.VMEM(rech.shape, jnp.float32), pltpu.SemaphoreType.DMA((3,))]
         + [padded, padded] + [field] * 8 + [padded, padded],
     )(cells, order, perm, rech, perm_far, rech_far)
     return exchange(send, rows // 2)

time: 55.7 us -> 55.7 us (level)
  no operation moved by 1% of the time
where the time goes in v7:
time: 55.7 us; the launch traced here: 55.5 us
  blocking collectives  44.6 us (80%)
  Pallas kernels  4.67 us (8%)
  starting transfers between devices  4.1 us (7%)
  waiting for transfers between devices  1.17 us (2%)
  between operations  0.69 us (1%)
    all_to_all x2, blocking collectives, stage(): lax.all_to_all(x.reshape(parts, -1, 1, columns), 'gx', split_axis=0, conc...  44.6 us
    ppermute x1, starting transfers between devices, body(): perm_far = lax.ppermute(perm, 'gy', swap)  3.33 us
    pallas_call x1, Pallas kernels, body(): call(stage_kernel, (f32(*perm.shape), f32(*recharge.shape), f32(2 * STEPS...  1.38 us
    pallas_call x1, Pallas kernels, body(): pl.pallas_call(apply_kernel, out_shape=(f32(*field), f32(*field)), in_spe...  1.34 us
    pallas_call x1, Pallas kernels, body(): mix = call(steps_kernel, f32(parts, parts), [VMEM] * 2)(known, own)  1.18 us
  transfers between devices with their start and end apart: 4, of which 2 were waited for; matrix products, arithmetic and copies ran while one was open for 0% of the time, Pallas kernels for 6%

profile of v7, /device:TPU:1, one launch (start us, length us, event | category | flops | bytes accessed | tf_op | source)
XLA Modules:
  0.0 55.5 jit_solution(8325973475215057871)
XLA Ops:
  0.6 3.3 %collective-permute-start = (f32[4,256,128]{2,1,0:T(8,128)}, f32[4,256,128]{2,1,0:T(8,128)S(1)}, u32[]{:S(2)}, u32[]{:S(2)}) collective-permute-start(f32[4,256,128]{2,1,0:T(8,128)} %bitcast.26), channel_id=1, source_target_pairs={{0,1},{1,0},{2,3},{3,2},{4,5},{5,4},{6,7},{7,6},{8,9},{9,8},{10,11... | collective-permute-start | bytes 1572872 | tf_op jit(solution)/shard_map/ppermute | solution.py:388
  4.0 0.1 collective-permute-start.1
  4.1 1.4 %shard_map.78 = (f32[4,256,128]{2,1,0:T(8,128)S(1)}, f32[4,256,128]{2,1,0:T(8,128)S(1)}, f32[16,128]{1,0:T(8,128)S(1)}) custom-call(f32[4,256,128]{2,1,0:T(8,128)} %bitcast.27, f32[4,256,128]{2,1,0:T(8,128)} %rech_any.1, s32[8]{0:T(128)} %order_any.1, f32[32]{0:T(128)} %obs_any.1, f32[32]{0:T(128)} %var_any.1), custom_call_target="tpu_custom_call" | custom-call | tf_op jit(solution)/shard_map/pallas_call | solution.py:394
  5.4 0.3 collective-permute-done
  5.7 45.3 %conditional.2 = (f32[2048,128]{1,0:T(8,128)S(1)}) conditional(s32[]{:T(128)} %convert_element_type.7, () %tuple.20, (f32[4,256,128]{2,1,0:T(8,128)S(1)}, f32[4,256,128]{2,1,0:T(8,128)S(1)}) %tuple.21), branch_computations={%region_0.0_spmd, %region_1.0_spmd} | conditional | bytes 8388616 | solution.py:400
  5.7 0.5 branch_1_fun.2
  6.2 24.0 %all_to_all.12 = f32[128,16,1,128]{3,1,2,0:T(8,128)S(1)} all-to-all(f32[128,16,1,128]{3,1,2,0:T(8,128)S(1)} %bitcast.20), channel_id=1, replica_groups={{0,32,64,96,128,160,192,224},{2,34,66,98,130,162,194,226},{4,36,68,100,..., dimensions={0} | all-to-all | bytes 2097152 | tf_op jit(solution)/shard_map/cond/branch_1_fun/all_to_all | solution.py:367
  30.3 0.1 copy.12
  30.4 20.6 %all_to_all.13 = f32[128,16,1,128]{3,1,2,0:T(8,128)S(1)} all-to-all(f32[128,16,1,128]{3,1,2,0:T(8,128)S(1)} %bitcast.24), channel_id=1, replica_groups={{0,2,4,6,8,10,12,14,16,18,20,22,24,26,28,30},{32,34,36,38,40,42,44,46,4..., dimensions={0} | all-to-all | bytes 2097152 | tf_op jit(solution)/shard_map/cond/branch_1_fun/all_to_all | solution.py:367
  50.9 0.1 copy.14
  51.0 0.0 collective-permute-done.1
  51.0 0.1 conditional.3
  51.0 0.1 concatenate.2
  51.2 0.2 shard_map.80
  51.4 0.1 collective-permute-start.2
  51.5 1.2 %shard_map.81.own_mix_ref = f32[128,128]{1,0:T(8,128)S(1)} custom-call(f32[16,128]{1,0:T(8,128)S(1)} %get-tuple-element.40.known_ref, f32[8,128]{1,0:T(8,128)S(1)} %shard_map.79.after_ref.own_ref), custom_call_target="tpu_custom_call" | custom-call | tf_op jit(solution)/shard_map/pallas_call | solution.py:408
  52.7 0.6 %collective-permute-start.3 = (f32[128,128]{1,0:T(8,128)S(1)}, f32[128,128]{1,0:T(8,128)S(1)}, u32[]{:S(2)}, u32[]{:S(2)}) collective-permute-start(f32[128,128]{1,0:T(8,128)S(1)} %shard_map.81.own_mix_ref), channel_id=1, source_target_pairs={{0,1},{1,0},{2,3},{3,2},{4,5},{5,4},{6,7},{7,6},{8,9},{9,8},{10,11... | collective-permute-start | bytes 196616 | tf_op jit(solution)/shard_map/ppermute | solution.py:411
  53.3 0.9 %collective-permute-done.3.other_mix_ref = f32[128,128]{1,0:T(8,128)S(1)} collective-permute-done((f32[128,128]{1,0:T(8,128)S(1)}, f32[128,128]{1,0:T(8,128)S(1)}, u32[]{:S(2)}, u32[]{:S(2)}) %collective-permute-start.3) | collective-permute-done | bytes 65568 | tf_op jit(solution)/shard_map/ppermute | solution.py:411
  54.2 0.0 collective-permute-done.2.got_ref
  54.2 1.3 %shard_map.82 = (f32[4,256,128]{2,1,0:T(8,128)}, f32[4,256,128]{2,1,0:T(8,128)}) custom-call(s32[1]{0:T(128)} %bitcast.15.core_ref, f32[2176,128]{1,0:T(8,128)S(1)} %get-tuple-element.46.recv_ref, f32[1024,128]{1,0:T(8,128)S(1)} %collective-permute-done.2.got_ref, f32[128,128]{1,0:T(8,128)S(1)} %shard_map.81.own_mix_ref, ...), custom_call_target="tpu_custom_call" | custom-call | tf_op jit(solution)/shard_map/pallas_call | solution.py:413
  (1 shorter events, 0.0 us)
Async XLA Ops:
  0.6 5.1 %collective-permute-start = (f32[4,256,128]{2,1,0:T(8,128)}, f32[4,256,128]{2,1,0:T(8,128)S(1)}, u32[]{:S(2)}, u32[]{:S(2)}) collective-permute-start(f32[4,256,128]{2,1,0:T(8,128)} %bitcast.26), channel_id=1, source_target_pairs={{0,1},{1,0},{2,3},{3,2},{4,5},{5,4},{6,7},{7,6},{8,9},{9,8},{10,11... | collective-permute-start | bytes 1572872 | tf_op jit(solution)/shard_map/ppermute | solution.py:388
  4.0 47.1 %collective-permute-start.1 = (f32[4,256,128]{2,1,0:T(8,128)}, f32[4,256,128]{2,1,0:T(8,128)}, u32[]{:S(2)}, u32[]{:S(2)}) collective-permute-start(f32[4,256,128]{2,1,0:T(8,128)} %rech_any.1), channel_id=1, source_target_pairs={{0,1},{1,0},{2,3},{3,2},{4,5},{5,4},{6,7},{7,6},{8,9},{9,8},{10,11... | collective-permute-start | bytes 1572872 | tf_op jit(solution)/shard_map/ppermute | solution.py:389
  51.4 2.8 %collective-permute-start.2 = (f32[1024,128]{1,0:T(8,128)S(1)}, f32[1024,128]{1,0:T(8,128)S(1)}, u32[]{:S(2)}, u32[]{:S(2)}) collective-permute-start(f32[1024,128]{1,0:T(8,128)S(1)} %shard_map.80), channel_id=1, source_target_pairs={{0,1},{1,0},{2,3},{3,2},{4,5},{5,4},{6,7},{7,6},{8,9},{9,8},{10,11... | collective-permute-start | bytes 1572872 | tf_op jit(solution)/shard_map/ppermute | solution.py:407
  52.7 1.5 %collective-permute-start.3 = (f32[128,128]{1,0:T(8,128)S(1)}, f32[128,128]{1,0:T(8,128)S(1)}, u32[]{:S(2)}, u32[]{:S(2)}) collective-permute-start(f32[128,128]{1,0:T(8,128)S(1)} %shard_map.81.own_mix_ref), channel_id=1, source_target_pairs={{0,1},{1,0},{2,3},{3,2},{4,5},{5,4},{6,7},{7,6},{8,9},{9,8},{10,11... | collective-permute-start | bytes 196616 | tf_op jit(solution)/shard_map/ppermute | solution.py:411

commit v8 on v6

--- a/solution.py
+++ b/solution.py
@@ -13,7 +13,7 @@
 LEAK = 0.1
 PAD = 8
 PLANE = 16
-CHUNK = 32
+CHUNK = 64
 HIGHEST = lax.Precision.HIGHEST
 
 VMEM = pl.BlockSpec(memory_space=pltpu.VMEM)

time: 55.7 us -> 55.8 us (level)
  no operation moved by 1% of the time
where the time goes in v8:
time: 55.8 us; the launch traced here: 55.6 us
  blocking collectives  44.6 us (80%)
  Pallas kernels  4.67 us (8%)
  starting transfers between devices  4.1 us (7%)
  waiting for transfers between devices  1.17 us (2%)
  between operations  0.69 us (1%)
    all_to_all x2, blocking collectives, stage(): lax.all_to_all(x.reshape(parts, -1, 1, columns), 'gx', split_axis=0, conc...  44.6 us
    ppermute x1, starting transfers between devices, body(): perm_far = lax.ppermute(perm, 'gy', swap)  3.33 us
    pallas_call x1, Pallas kernels, body(): call(stage_kernel, (f32(*perm.shape), f32(*recharge.shape), f32(2 * STEPS...  1.38 us
    pallas_call x1, Pallas kernels, body(): pl.pallas_call(apply_kernel, out_shape=(f32(*field), f32(*field)), in_spe...  1.34 us
    pallas_call x1, Pallas kernels, body(): mix = call(steps_kernel, f32(parts, parts), [VMEM] * 2)(known, own)  1.18 us
  transfers between devices with their start and end apart: 4, of which 2 were waited for; matrix products, arithmetic and copies ran while one was open for 0% of the time, Pallas kernels for 6%

profile of v8, /device:TPU:1, one launch (start us, length us, event | category | flops | bytes accessed | tf_op | source)
XLA Modules:
  0.0 55.6 jit_solution(2793814068219624660)
XLA Ops:
  0.6 3.3 %collective-permute-start = (f32[4,256,128]{2,1,0:T(8,128)}, f32[4,256,128]{2,1,0:T(8,128)S(1)}, u32[]{:S(2)}, u32[]{:S(2)}) collective-permute-start(f32[4,256,128]{2,1,0:T(8,128)} %bitcast.26), channel_id=1, source_target_pairs={{0,1},{1,0},{2,3},{3,2},{4,5},{5,4},{6,7},{7,6},{8,9},{9,8},{10,11... | collective-permute-start | bytes 1572872 | tf_op jit(solution)/shard_map/ppermute | solution.py:383
  4.0 0.1 collective-permute-start.1
  4.1 1.4 %shard_map.78 = (f32[4,256,128]{2,1,0:T(8,128)S(1)}, f32[4,256,128]{2,1,0:T(8,128)S(1)}, f32[16,128]{1,0:T(8,128)S(1)}) custom-call(f32[4,256,128]{2,1,0:T(8,128)} %bitcast.27, f32[4,256,128]{2,1,0:T(8,128)} %rech_any.1, s32[8]{0:T(128)} %order_any.1, f32[32]{0:T(128)} %obs_any.1, f32[32]{0:T(128)} %var_any.1), custom_call_target="tpu_custom_call" | custom-call | tf_op jit(solution)/shard_map/pallas_call | solution.py:389
  5.4 0.3 collective-permute-done
  5.7 45.4 %conditional.2 = (f32[2048,128]{1,0:T(8,128)S(1)}) conditional(s32[]{:T(128)} %convert_element_type.7, () %tuple.20, (f32[4,256,128]{2,1,0:T(8,128)S(1)}, f32[4,256,128]{2,1,0:T(8,128)S(1)}) %tuple.21), branch_computations={%region_0.0_spmd, %region_1.0_spmd} | conditional | bytes 8388616 | solution.py:395
  5.7 0.5 branch_1_fun.2
  6.2 24.0 %all_to_all.12 = f32[128,16,1,128]{3,1,2,0:T(8,128)S(1)} all-to-all(f32[128,16,1,128]{3,1,2,0:T(8,128)S(1)} %bitcast.20), channel_id=1, replica_groups={{0,32,64,96,128,160,192,224},{2,34,66,98,130,162,194,226},{4,36,68,100,..., dimensions={0} | all-to-all | bytes 2097152 | tf_op jit(solution)/shard_map/cond/branch_1_fun/all_to_all | solution.py:362
  30.3 0.1 copy.12
  30.4 20.6 %all_to_all.13 = f32[128,16,1,128]{3,1,2,0:T(8,128)S(1)} all-to-all(f32[128,16,1,128]{3,1,2,0:T(8,128)S(1)} %bitcast.24), channel_id=1, replica_groups={{0,2,4,6,8,10,12,14,16,18,20,22,24,26,28,30},{32,34,36,38,40,42,44,46,4..., dimensions={0} | all-to-all | bytes 2097152 | tf_op jit(solution)/shard_map/cond/branch_1_fun/all_to_all | solution.py:362
  51.0 0.1 copy.14
  51.1 0.0 collective-permute-done.1
  51.1 0.1 conditional.3
  51.1 0.1 concatenate.2
  51.3 0.2 shard_map.80
  51.5 0.1 collective-permute-start.2
  51.6 1.2 %shard_map.81.own_mix_ref = f32[128,128]{1,0:T(8,128)S(1)} custom-call(f32[16,128]{1,0:T(8,128)S(1)} %get-tuple-element.40.known_ref, f32[8,128]{1,0:T(8,128)S(1)} %shard_map.79.after_ref.own_ref), custom_call_target="tpu_custom_call" | custom-call | tf_op jit(solution)/shard_map/pallas_call | solution.py:403
  52.8 0.6 %collective-permute-start.3 = (f32[128,128]{1,0:T(8,128)S(1)}, f32[128,128]{1,0:T(8,128)S(1)}, u32[]{:S(2)}, u32[]{:S(2)}) collective-permute-start(f32[128,128]{1,0:T(8,128)S(1)} %shard_map.81.own_mix_ref), channel_id=1, source_target_pairs={{0,1},{1,0},{2,3},{3,2},{4,5},{5,4},{6,7},{7,6},{8,9},{9,8},{10,11... | collective-permute-start | bytes 196616 | tf_op jit(solution)/shard_map/ppermute | solution.py:406
  53.3 0.9 %collective-permute-done.3.other_mix_ref = f32[128,128]{1,0:T(8,128)S(1)} collective-permute-done((f32[128,128]{1,0:T(8,128)S(1)}, f32[128,128]{1,0:T(8,128)S(1)}, u32[]{:S(2)}, u32[]{:S(2)}) %collective-permute-start.3) | collective-permute-done | bytes 65568 | tf_op jit(solution)/shard_map/ppermute | solution.py:406
  54.2 0.0 collective-permute-done.2.got_ref
  54.3 1.3 %shard_map.82 = (f32[4,256,128]{2,1,0:T(8,128)}, f32[4,256,128]{2,1,0:T(8,128)}) custom-call(s32[1]{0:T(128)} %bitcast.15.core_ref, f32[2176,128]{1,0:T(8,128)S(1)} %get-tuple-element.46.recv_ref, f32[1024,128]{1,0:T(8,128)S(1)} %collective-permute-done.2.got_ref, f32[128,128]{1,0:T(8,128)S(1)} %shard_map.81.own_mix_ref, ...), custom_call_target="tpu_custom_call" | custom-call | tf_op jit(solution)/shard_map/pallas_call | solution.py:408
  (1 shorter events, 0.0 us)
Async XLA Ops:
  0.6 5.1 %collective-permute-start = (f32[4,256,128]{2,1,0:T(8,128)}, f32[4,256,128]{2,1,0:T(8,128)S(1)}, u32[]{:S(2)}, u32[]{:S(2)}) collective-permute-start(f32[4,256,128]{2,1,0:T(8,128)} %bitcast.26), channel_id=1, source_target_pairs={{0,1},{1,0},{2,3},{3,2},{4,5},{5,4},{6,7},{7,6},{8,9},{9,8},{10,11... | collective-permute-start | bytes 1572872 | tf_op jit(solution)/shard_map/ppermute | solution.py:383
  4.0 47.2 %collective-permute-start.1 = (f32[4,256,128]{2,1,0:T(8,128)}, f32[4,256,128]{2,1,0:T(8,128)}, u32[]{:S(2)}, u32[]{:S(2)}) collective-permute-start(f32[4,256,128]{2,1,0:T(8,128)} %rech_any.1), channel_id=1, source_target_pairs={{0,1},{1,0},{2,3},{3,2},{4,5},{5,4},{6,7},{7,6},{8,9},{9,8},{10,11... | collective-permute-start | bytes 1572872 | tf_op jit(solution)/shard_map/ppermute | solution.py:384
  51.5 2.8 %collective-permute-start.2 = (f32[1024,128]{1,0:T(8,128)S(1)}, f32[1024,128]{1,0:T(8,128)S(1)}, u32[]{:S(2)}, u32[]{:S(2)}) collective-permute-start(f32[1024,128]{1,0:T(8,128)S(1)} %shard_map.80), channel_id=1, source_target_pairs={{0,1},{1,0},{2,3},{3,2},{4,5},{5,4},{6,7},{7,6},{8,9},{9,8},{10,11... | collective-permute-start | bytes 1572872 | tf_op jit(solution)/shard_map/ppermute | solution.py:402
  52.8 1.5 %collective-permute-start.3 = (f32[128,128]{1,0:T(8,128)S(1)}, f32[128,128]{1,0:T(8,128)S(1)}, u32[]{:S(2)}, u32[]{:S(2)}) collective-permute-start(f32[128,128]{1,0:T(8,128)S(1)} %shard_map.81.own_mix_ref), channel_id=1, source_target_pairs={{0,1},{1,0},{2,3},{3,2},{4,5},{5,4},{6,7},{7,6},{8,9},{9,8},{10,11... | collective-permute-start | bytes 196616 | tf_op jit(solution)/shard_map/ppermute | solution.py:406
